TPU v7x, 128 devices: a whole 4x4x4 slice. The times are simulated.
128 devices in a mesh: section: 8 (over z, y_lo), ctx: 8 (over x, core), tp: 2 (over y_hi).
Axes of the slice: x: 4, y: 4 (y_hi: 2, y_lo: 2; y = y_hi * 2 + y_lo), z: 4, core: 2. Of those that a mesh axis runs over, the one named last changes fastest.
Arguments:
- queries: bfloat16 [8, 1024, 8192], P('section', 'ctx', 'tp'), may hold values from -6 to 6
- span_keys: bfloat16 [8, 1024, 512], P('section', ('ctx', 'tp')), may hold values from -6 to 6
- span_values: bfloat16 [8, 1024, 512], P('section', ('ctx', 'tp')), may hold values from -6 to 6
- prefix_keys: bfloat16 [8, 6144, 512], P('section', ('ctx', 'tp')), may hold values from -6 to 6
- prefix_values: bfloat16 [8, 6144, 512], P('section', ('ctx', 'tp')), may hold values from -6 to 6
- out_weight: bfloat16 [8, 8192, 8192], P('section', 'tp', 'ctx'), may hold values from -0.375 to 0.375
- residual: bfloat16 [8, 1024, 8192], P('section', 'tp', 'ctx'), may hold values from -6 to 6
- block_slot: int32 [48], replicated, may hold values from 0 to 47, each once
- span_index: int32 [8], P('section'), may hold values from 3 to 6
Outputs:
- handoff: bfloat16 [8, 1024, 8192], P('section', 'tp', 'ctx')
Inputs may be any that keep to these rules, and one draw needn't show every extreme that they name: `block_slot`: each page number appears once.
All inputs are finite; a program needn't handle non-finite values.
Results may differ from a plain program's by a relative error of at most 0.015.
Values may be sent and summed in bfloat16 or wider, within the bound.
A program may use at most 128 MiB of HBM per device.

v0:
```python
import math

import jax
import jax.numpy as jnp
from jax import lax
from jax.sharding import PartitionSpec as P

KVH = 4
HD = 128
BLK = 128


NEGATIVE = -1e30


def from_behind(value, axis, by):
    length = lax.axis_size(axis)
    return lax.ppermute(value, axis, [(i, (i + by) % length) for i in range(length)])


def attend(softmax_state, grouped, key_rows, value_rows, visible, score_scale):
    running_max, running_sum, weighted = softmax_state
    row_count = key_rows.shape[0]
    kv_local = grouped.shape[1]
    keyed = key_rows.reshape(row_count, kv_local, HD)
    valued = value_rows.reshape(row_count, kv_local, HD)
    scores = (
        jnp.einsum("rkd,qkgd->kgrq", keyed, grouped, preferred_element_type=jnp.float32)
        * score_scale
    )
    scores = jnp.where(visible[None, None], scores, NEGATIVE)
    new_max = jnp.maximum(running_max, jnp.max(scores, axis=2))
    rescale = jnp.exp(running_max - new_max)
    weights = jnp.where(visible[None, None], jnp.exp(scores - new_max[:, :, None, :]), 0.0)
    running_sum = running_sum * rescale + jnp.sum(weights, axis=2)
    update = jnp.einsum(
        "kgrq,rkd->qkgd", weights.astype(jnp.bfloat16), valued, preferred_element_type=jnp.float32
    )
    weighted = weighted * jnp.transpose(rescale, (2, 0, 1))[..., None] + update
    return (new_max, running_sum, weighted)


def make_fold(grouped, block_slot, page_limit, query_pos, prefix_rows, span_rows):
    shard_rows = prefix_rows + span_rows
    pages_per = prefix_rows // BLK
    score_scale = 1.0 / math.sqrt(HD)
    query_count = query_pos.shape[0]

    def cache_fold(softmax_state, gathered, start_row):
        key_rows, value_rows = gathered
        columns = key_rows.shape[1]
        shard_count = key_rows.shape[0] // shard_rows
        key_rows = key_rows.reshape(shard_count, shard_rows, columns)
        value_rows = value_rows.reshape(shard_count, shard_rows, columns)

        def per_shard(shard_state, shard_item):
            shard_keys, shard_values, shard_number = shard_item
            page_slots = lax.dynamic_slice_in_dim(block_slot, shard_number * pages_per, pages_per)
            page_keys = shard_keys[:prefix_rows].reshape(pages_per, BLK, columns)
            page_values = shard_values[:prefix_rows].reshape(pages_per, BLK, columns)

            def per_page(inner_state, page_item):
                page_key, page_value, page_slot = page_item
                allowed = page_slot < page_limit
                visible = jnp.broadcast_to(allowed, (BLK, query_count))
                inner_state = attend(
                    inner_state, grouped, page_key, page_value, visible, score_scale
                )
                return (inner_state, None)

            shard_state, _ = lax.scan(per_page, shard_state, (page_keys, page_values, page_slots))
            span_pos = shard_number * span_rows + jnp.arange(span_rows, dtype=jnp.int32)
            visible = span_pos[:, None] <= query_pos[None, :]
            shard_state = attend(
                shard_state,
                grouped,
                shard_keys[prefix_rows:],
                shard_values[prefix_rows:],
                visible,
                score_scale,
            )
            return (shard_state, None)

        numbers = jnp.arange(shard_count, dtype=jnp.int32)
        softmax_state, _ = lax.scan(per_shard, softmax_state, (key_rows, value_rows, numbers))
        return softmax_state

    return cache_fold


def per_device(
    queries,
    span_keys,
    span_values,
    prefix_keys,
    prefix_values,
    out_weight,
    residual,
    block_slot,
    span_index,
):
    query_rows = queries.shape[1]
    local_heads = queries.shape[2] // HD
    kv_local = KVH // lax.axis_size("tp")
    group_size = local_heads // kv_local
    grouped = queries[0].reshape(query_rows, kv_local, group_size, HD)
    span_length = query_rows * lax.axis_size("ctx")
    page_limit = span_index[0] * (span_length // BLK)
    query_pos = lax.axis_index("ctx") * query_rows + jnp.arange(query_rows, dtype=jnp.int32)
    prefix_rows = prefix_keys.shape[1]
    span_rows = span_keys.shape[1]
    cache_keys = jnp.concatenate([prefix_keys[0], span_keys[0]], axis=0)
    cache_values = jnp.concatenate([prefix_values[0], span_values[0]], axis=0)
    cache_fold = make_fold(grouped, block_slot, page_limit, query_pos, prefix_rows, span_rows)
    initial = (
        jnp.full((kv_local, group_size, query_rows), NEGATIVE, jnp.float32),
        jnp.zeros((kv_local, group_size, query_rows), jnp.float32),
        jnp.zeros((query_rows, kv_local, group_size, HD), jnp.float32),
    )
    head_start = lax.axis_index("tp") * (kv_local * HD)
    key_rows = lax.dynamic_slice_in_dim(
        lax.all_gather(cache_keys, ("ctx", "tp"), axis=0, tiled=True), head_start, kv_local * HD, 1
    )
    value_rows = lax.dynamic_slice_in_dim(
        lax.all_gather(cache_values, ("ctx", "tp"), axis=0, tiled=True),
        head_start,
        kv_local * HD,
        1,
    )
    softmax_state = cache_fold(initial, (key_rows, value_rows), jnp.int32(0))
    running_sum = softmax_state[1]
    weighted = softmax_state[2]
    heads = (
        (weighted / jnp.transpose(running_sum, (2, 0, 1))[..., None])
        .reshape(query_rows, local_heads * HD)
        .astype(jnp.bfloat16)
    )
    weight_local = out_weight[0]
    partial_terms = jnp.dot(
        lax.all_gather(heads, "ctx", axis=0, tiled=True),
        weight_local,
        preferred_element_type=jnp.float32,
    )
    summed = lax.psum_scatter(
        partial_terms.astype(jnp.bfloat16), "tp", scatter_dimension=0, tiled=True
    ).astype(jnp.float32)
    layer = (residual[0].astype(jnp.float32) + summed).astype(jnp.bfloat16)
    handed = from_behind(layer, "section", 1)
    return handed[None]


def solution(mesh):
    in_specs = (
        P("section", "ctx", "tp"),
        P("section", ("ctx", "tp"), None),
        P("section", ("ctx", "tp"), None),
        P("section", ("ctx", "tp"), None),
        P("section", ("ctx", "tp"), None),
        P("section", "tp", "ctx"),
        P("section", "tp", "ctx"),
        P(),
        P("section"),
    )
    out_specs = P("section", "tp", "ctx")
    return jax.shard_map(
        per_device, mesh=mesh, in_specs=in_specs, out_specs=out_specs, check_vma=False
    )
```

profile of v0, /device:TPU:1, one launch (start us, length us, event | category | flops | bytes accessed | tf_op | source)
XLA Modules:
  0.0 905.0 jit_solution(4819985830013118573)
XLA Ops:
  12.5 69.5 %all-gather.4.cloned.1.call-done = bf16[7168,512]{1,0:T(8,128)(2,1)} async-done(((bf16[448,512]{1,0:T(8,128)(2,1)}), bf16[7168,512]{1,0:T(8,128)(2,1)}) %all-gather.4.cloned.1.call-update) | async-done | bytes 7340048 | tf_op jit(solution)/shard_map/all_gather | solution.py:122
  86.1 64.8 %all-gather.6.cloned.1.call-done = bf16[7168,512]{1,0:T(8,128)(2,1)} async-done(((bf16[448,512]{1,0:T(8,128)(2,1)}), bf16[7168,512]{1,0:T(8,128)(2,1)}) %all-gather.6.cloned.1.call-update) | async-done | bytes 7340048 | tf_op jit(solution)/shard_map/all_gather | solution.py:125
  150.9 4.2 constant_dynamic-slice_fusion.6
  155.6 607.9 %while.31 = (s32[]{:T(128)}, f32[2,16,128]{2,1,0:T(8,128)S(1)}, f32[2,16,128]{2,1,0:T(8,128)S(1)}, f32[128,2,16,128]{0,3,2,1:T(8,128)}, bf16[16,448,256]{2,1,0:T...) while((s32[]{:T(128)}, f32[2,16,128]{2,1,0:T(8,128)S(1)}, ...), condition=%wide.region_7.8_spmd.clone, body=%wide.region_0.7_spmd.clone.sunk | while | flops 414490816 | bytes 39061568 | solution.py:85
  162.0 23.6 %while.32 = (s32[]{:T(128)}, f32[2,16,128]{2,1,0:T(8,128)S(1)}, f32[2,16,128]{2,1,0:T(8,128)S(1)}, f32[128,2,16,128]{0,3,2,1:T(8,128)}, s32[3]{0:T(128)}, /*inde...) while((s32[]{:T(128)}, f32[2,16,128]{2,1,0:T(8,128)S(1)}, ...), condition=%wide.region_4.4_spmd, body=%wide.region_1.3_spmd.sunk | while | flops 276312064 | bytes 12451969 | solution.py:71
  200.1 23.6 %while.32 = (s32[]{:T(128)}, f32[2,16,128]{2,1,0:T(8,128)S(1)}, f32[2,16,128]{2,1,0:T(8,128)S(1)}, f32[128,2,16,128]{0,3,2,1:T(8,128)}, s32[3]{0:T(128)}, /*inde...) while((s32[]{:T(128)}, f32[2,16,128]{2,1,0:T(8,128)S(1)}, ...), condition=%wide.region_4.4_spmd, body=%wide.region_1.3_spmd.sunk | while | flops 276312064 | bytes 12451969 | solution.py:71
  238.2 23.6 %while.32 = (s32[]{:T(128)}, f32[2,16,128]{2,1,0:T(8,128)S(1)}, f32[2,16,128]{2,1,0:T(8,128)S(1)}, f32[128,2,16,128]{0,3,2,1:T(8,128)}, s32[3]{0:T(128)}, /*inde...) while((s32[]{:T(128)}, f32[2,16,128]{2,1,0:T(8,128)S(1)}, ...), condition=%wide.region_4.4_spmd, body=%wide.region_1.3_spmd.sunk | while | flops 276312064 | bytes 12451969 | solution.py:71
  276.3 23.6 %while.32 = (s32[]{:T(128)}, f32[2,16,128]{2,1,0:T(8,128)S(1)}, f32[2,16,128]{2,1,0:T(8,128)S(1)}, f32[128,2,16,128]{0,3,2,1:T(8,128)}, s32[3]{0:T(128)}, /*inde...) while((s32[]{:T(128)}, f32[2,16,128]{2,1,0:T(8,128)S(1)}, ...), condition=%wide.region_4.4_spmd, body=%wide.region_1.3_spmd.sunk | while | flops 276312064 | bytes 12451969 | solution.py:71
  314.4 23.6 %while.32 = (s32[]{:T(128)}, f32[2,16,128]{2,1,0:T(8,128)S(1)}, f32[2,16,128]{2,1,0:T(8,128)S(1)}, f32[128,2,16,128]{0,3,2,1:T(8,128)}, s32[3]{0:T(128)}, /*inde...) while((s32[]{:T(128)}, f32[2,16,128]{2,1,0:T(8,128)S(1)}, ...), condition=%wide.region_4.4_spmd, body=%wide.region_1.3_spmd.sunk | while | flops 276312064 | bytes 12451969 | solution.py:71
  352.5 23.6 %while.32 = (s32[]{:T(128)}, f32[2,16,128]{2,1,0:T(8,128)S(1)}, f32[2,16,128]{2,1,0:T(8,128)S(1)}, f32[128,2,16,128]{0,3,2,1:T(8,128)}, s32[3]{0:T(128)}, /*inde...) while((s32[]{:T(128)}, f32[2,16,128]{2,1,0:T(8,128)S(1)}, ...), condition=%wide.region_4.4_spmd, body=%wide.region_1.3_spmd.sunk | while | flops 276312064 | bytes 12451969 | solution.py:71
  390.6 23.6 %while.32 = (s32[]{:T(128)}, f32[2,16,128]{2,1,0:T(8,128)S(1)}, f32[2,16,128]{2,1,0:T(8,128)S(1)}, f32[128,2,16,128]{0,3,2,1:T(8,128)}, s32[3]{0:T(128)}, /*inde...) while((s32[]{:T(128)}, f32[2,16,128]{2,1,0:T(8,128)S(1)}, ...), condition=%wide.region_4.4_spmd, body=%wide.region_1.3_spmd.sunk | while | flops 276312064 | bytes 12451969 | solution.py:71
  428.7 23.6 %while.32 = (s32[]{:T(128)}, f32[2,16,128]{2,1,0:T(8,128)S(1)}, f32[2,16,128]{2,1,0:T(8,128)S(1)}, f32[128,2,16,128]{0,3,2,1:T(8,128)}, s32[3]{0:T(128)}, /*inde...) while((s32[]{:T(128)}, f32[2,16,128]{2,1,0:T(8,128)S(1)}, ...), condition=%wide.region_4.4_spmd, body=%wide.region_1.3_spmd.sunk | while | flops 276312064 | bytes 12451969 | solution.py:71
  466.8 23.6 %while.32 = (s32[]{:T(128)}, f32[2,16,128]{2,1,0:T(8,128)S(1)}, f32[2,16,128]{2,1,0:T(8,128)S(1)}, f32[128,2,16,128]{0,3,2,1:T(8,128)}, s32[3]{0:T(128)}, /*inde...) while((s32[]{:T(128)}, f32[2,16,128]{2,1,0:T(8,128)S(1)}, ...), condition=%wide.region_4.4_spmd, body=%wide.region_1.3_spmd.sunk | while | flops 276312064 | bytes 12451969 | solution.py:71
  504.9 23.6 %while.32 = (s32[]{:T(128)}, f32[2,16,128]{2,1,0:T(8,128)S(1)}, f32[2,16,128]{2,1,0:T(8,128)S(1)}, f32[128,2,16,128]{0,3,2,1:T(8,128)}, s32[3]{0:T(128)}, /*inde...) while((s32[]{:T(128)}, f32[2,16,128]{2,1,0:T(8,128)S(1)}, ...), condition=%wide.region_4.4_spmd, body=%wide.region_1.3_spmd.sunk | while | flops 276312064 | bytes 12451969 | solution.py:71
  543.0 23.6 %while.32 = (s32[]{:T(128)}, f32[2,16,128]{2,1,0:T(8,128)S(1)}, f32[2,16,128]{2,1,0:T(8,128)S(1)}, f32[128,2,16,128]{0,3,2,1:T(8,128)}, s32[3]{0:T(128)}, /*inde...) while((s32[]{:T(128)}, f32[2,16,128]{2,1,0:T(8,128)S(1)}, ...), condition=%wide.region_4.4_spmd, body=%wide.region_1.3_spmd.sunk | while | flops 276312064 | bytes 12451969 | solution.py:71
  581.1 23.6 %while.32 = (s32[]{:T(128)}, f32[2,16,128]{2,1,0:T(8,128)S(1)}, f32[2,16,128]{2,1,0:T(8,128)S(1)}, f32[128,2,16,128]{0,3,2,1:T(8,128)}, s32[3]{0:T(128)}, /*inde...) while((s32[]{:T(128)}, f32[2,16,128]{2,1,0:T(8,128)S(1)}, ...), condition=%wide.region_4.4_spmd, body=%wide.region_1.3_spmd.sunk | while | flops 276312064 | bytes 12451969 | solution.py:71
  619.2 23.6 %while.32 = (s32[]{:T(128)}, f32[2,16,128]{2,1,0:T(8,128)S(1)}, f32[2,16,128]{2,1,0:T(8,128)S(1)}, f32[128,2,16,128]{0,3,2,1:T(8,128)}, s32[3]{0:T(128)}, /*inde...) while((s32[]{:T(128)}, f32[2,16,128]{2,1,0:T(8,128)S(1)}, ...), condition=%wide.region_4.4_spmd, body=%wide.region_1.3_spmd.sunk | while | flops 276312064 | bytes 12451969 | solution.py:71
  657.3 23.6 %while.32 = (s32[]{:T(128)}, f32[2,16,128]{2,1,0:T(8,128)S(1)}, f32[2,16,128]{2,1,0:T(8,128)S(1)}, f32[128,2,16,128]{0,3,2,1:T(8,128)}, s32[3]{0:T(128)}, /*inde...) while((s32[]{:T(128)}, f32[2,16,128]{2,1,0:T(8,128)S(1)}, ...), condition=%wide.region_4.4_spmd, body=%wide.region_1.3_spmd.sunk | while | flops 276312064 | bytes 12451969 | solution.py:71
  695.4 23.6 %while.32 = (s32[]{:T(128)}, f32[2,16,128]{2,1,0:T(8,128)S(1)}, f32[2,16,128]{2,1,0:T(8,128)S(1)}, f32[128,2,16,128]{0,3,2,1:T(8,128)}, s32[3]{0:T(128)}, /*inde...) while((s32[]{:T(128)}, f32[2,16,128]{2,1,0:T(8,128)S(1)}, ...), condition=%wide.region_4.4_spmd, body=%wide.region_1.3_spmd.sunk | while | flops 276312064 | bytes 12451969 | solution.py:71
  733.5 23.6 %while.32 = (s32[]{:T(128)}, f32[2,16,128]{2,1,0:T(8,128)S(1)}, f32[2,16,128]{2,1,0:T(8,128)S(1)}, f32[128,2,16,128]{0,3,2,1:T(8,128)}, s32[3]{0:T(128)}, /*inde...) while((s32[]{:T(128)}, f32[2,16,128]{2,1,0:T(8,128)S(1)}, ...), condition=%wide.region_4.4_spmd, body=%wide.region_1.3_spmd.sunk | while | flops 276312064 | bytes 12451969 | solution.py:71
  766.5 51.9 %all-gather.8.cloned.1.call-done = bf16[1024,4096]{0,1:T(8,128)(2,1)} async-done(((bf16[128,4096]{0,1:T(8,128)(2,1)}), bf16[1024,4096]{0,1:T(8,128)(2,1)}) %all-gather.8.cloned.1.call-update) | async-done | bytes 8388624 | tf_op jit(solution)/shard_map/all_gather | solution.py:140
  818.4 14.7 %fusion.32 = bf16[1024,1024]{1,0:T(8,128)(2,1)} fusion(bf16[1024,4096]{0,1:T(8,128)(2,1)} %all-gather.8.cloned.1.call-done, bf16[1,4096,1024]{2,1,0:T(8,128)(2,1)} %param.18), kind=kOutput, calls=%fused_computation.54 | convolution fusion | flops 8590983168 | bytes 18874368 | tf_op jit(solution)/shard_map/dot_general | solution.py:139
  833.2 36.6 %reduce-scatter.2.cloned.1.call-done = bf16[512,1024]{1,0:T(8,128)(2,1)} async-done(((bf16[1024,1024]{1,0:T(8,128)(2,1)}), bf16[512,1024]{1,0:T(8,128)(2,1)}) %reduce-scatter.2.cloned.1.call-update) | async-done | bytes 1048592 | tf_op jit(solution)/shard_map/reduce_scatter | solution.py:144
  871.7 25.8 %collective-permute-done = bf16[512,1024]{1,0:T(8,128)(2,1)S(1)} collective-permute-done((bf16[512,1024]{1,0:T(8,128)(2,1)S(1)}, bf16[512,1024]{1,0:T(8,128)(2,1)S(1)}, u32[]{:S(2)}, u32[]{:S(2)}) %collective-permute-start) | collective-permute-done | bytes 1048608 | tf_op jit(solution)/shard_map/ppermute | solution.py:18
  (825 shorter events, 569.2 us)
Async XLA Ops:
  6.5 3.9 copy-start.3
  6.5 75.5 %all-gather.4.cloned.1.call-start = ((), (), s32[]{:S(2)}) async-start(), calls=%async_computation.1 | async-start | bytes 7798784 | tf_op jit(solution)/shard_map/all_gather | solution.py:122
  8.5 142.4 %all-gather.6.cloned.1.call-start = ((), (), s32[]{:S(2)}) async-start(), calls=%async_computation.2 | async-start | bytes 7798784 | tf_op jit(solution)/shard_map/all_gather | solution.py:125
  10.4 808.0 %all-gather.8.cloned.1.call-start = ((), (), s32[]{:S(2)}) async-start(), calls=%async_computation.3 | async-start | bytes 9437184 | tf_op jit(solution)/shard_map/all_gather | solution.py:140
  185.6 3.1 copy-start
  188.7 3.1 copy-start.1
  226.8 3.1 copy-start.1
  264.9 3.1 copy-start.1
  303.0 3.1 copy-start.1
  341.1 3.1 copy-start.1
  379.2 3.1 copy-start.1
  417.3 3.1 copy-start.1
  455.4 3.1 copy-start.1
  493.5 3.1 copy-start.1
  531.6 3.1 copy-start.1
  569.7 3.1 copy-start.1
  607.8 3.1 copy-start.1
  645.9 3.1 copy-start.1
  684.0 3.1 copy-start.1
  722.1 3.1 copy-start.1
  760.2 3.1 copy-start.1
  766.4 103.3 %reduce-scatter.2.cloned.1.call-start = ((), (), s32[]{:S(2)}) async-start(), calls=%async_computation.4 | async-start | bytes 3145728 | tf_op jit(solution)/shard_map/reduce_scatter | solution.py:144
  833.1 36.6 %copy-start.2 = (bf16[1,512,1024]{2,1,0:T(8,128)(2,1)S(1)}, bf16[1,512,1024]{2,1,0:T(8,128)(2,1)}, u32[]{:S(2)}) copy-start(bf16[1,512,1024]{2,1,0:T(8,128)(2,1)} %param.19) | copy-start | bytes 3145732
  871.4 26.2 %collective-permute-start = (bf16[512,1024]{1,0:T(8,128)(2,1)S(1)}, bf16[512,1024]{1,0:T(8,128)(2,1)S(1)}, u32[]{:S(2)}, u32[]{:S(2)}) collective-permute-start(bf16[512,1024]{1,0:T(8,128)(2,1)S(1)} %fusion.31), channel_id=1, source_target_pairs={{0,16},{16,32},{32,48},{48,64},{64,80},{80,96},{96,112},{112,0},{1... | collective-permute-start | bytes 3145736 | tf_op jit(solution)/shard_map/ppermute | solution.py:18
  (15 other events, 46.8 us)
Sparse Core Ops, SparseCore 0:
  9.8 72.1 all-gather.3
  84.4 66.4 all-gather.5
  766.6 51.7 all-gather.7
  833.3 36.4 reduce-scatter.1
where the time goes:
time: 912 us; the launch traced here: 905 us
  matrix products  293 us (32%)
  waiting for transfers between devices  249 us (27%)
  local copies, waits for them, and re-layouts  204 us (22%)
  other arithmetic  90 us (10%)
  loops' own time  54.5 us (6%)
  between operations  13.9 us (2%)
    dot_general x64, matrix products, attend(): jnp.einsum('kgrq,rkd->qkgd', weights.astype(jnp.bfloat16), valued, prefer...  230 us
    dynamic_slice x192, local copies, waits for them, and re-layouts, per_shard(): lax.scan(per_page, shard_state, (page_keys, page_values, page_slots))  113 us
    all_gather x1, waiting for transfers between devices, per_device(): lax.all_gather(cache_keys, ('ctx', 'tp'), axis=0, tiled=True)  69.5 us
    all_gather x1, waiting for transfers between devices, per_device(): lax.all_gather(cache_values, ('ctx', 'tp'), axis=0, tiled=True)  64.8 us
    all_gather x1, waiting for transfers between devices, per_device(): lax.all_gather(heads, 'ctx', axis=0, tiled=True)  51.9 us
    while x32, other arithmetic  49.5 us
    dot_general x64, matrix products, attend(): jnp.einsum('rkd,qkgd->kgrq', keyed, grouped, preferred_element_type=jnp.f...  48.2 us
    reduce_scatter x1, waiting for transfers between devices, per_device(): lax.psum_scatter(partial_terms.astype(jnp.bfloat16), 'tp', scatter_dimens...  36.6 us
  transfers between devices with their start and end apart: 5, of which 5 were waited for; matrix products, arithmetic and copies ran while one was open for 1% of the time, Pallas kernels for 0%

commit v1 on v0

v1 whole, which is shorter than its diff:
```python
import functools
import math

import jax
import jax.numpy as jnp
from jax import lax
from jax.experimental import pallas as pl
from jax.experimental.pallas import tpu as pltpu
from jax.sharding import PartitionSpec as P

MESH = pl.DeviceIdType.MESH
HD = 128
BLK = 128
QB = 1024
PRE = 384
SPN = 64
SLOT = 2 * PRE
SPAN = 1024
VR = 144
LOW = -1e30
SOURCES = ((0, 0), (1, 0), (3, 0), (0, 1), (1, 1), (3, 1), (2, 0), (2, 1))


def where_am_i():
    ctx = lax.axis_index("ctx")
    return lax.axis_index("section"), ctx // 2, lax.rem(ctx, 2), lax.axis_index("tp")


def pick(index, table):
    value = jnp.int32(table[-1])
    for position in range(len(table) - 1):
        value = jnp.where(index == position, jnp.int32(table[position]), value)
    return value


def attention_kernel(
    q_hbm, sk_hbm, sv_hbm, pk_hbm, pv_hbm, slot_ref, limit_ref, heads_ref,
    kv, q_raw, q_t, k_two, v_t, ks_two, vs_raw, vs_t, scores, span_scores, tri, block_max, row_max, acc,
    send_sem, recv_sem, fwd_send, fwd_recv, q_send, q_recv, local_sem,
):
    section, x, core, tp = where_am_i()
    swap_x = 3 - x

    def device(dx, dt):
        return (section, lax.rem(x + dx, 4) * 2 + core, lax.rem(tp + dt, 2))

    sibling = (section, x * 2 + 1 - core, tp)
    swap_device = (section, swap_x * 2 + core, tp)

    barrier = pltpu.get_barrier_semaphore()
    for dx, dt in SOURCES[1:]:
        pl.semaphore_signal(barrier, inc=1, device_id=device(dx, dt), device_id_type=MESH)
    pl.semaphore_signal(barrier, inc=1, device_id=sibling, device_id_type=MESH)

    def own_parts(head):
        cols = pl.ds(pl.multiple_of(head * HD, HD), HD)
        return (
            (pk_hbm.at[:, cols], 0, 0, PRE),
            (pv_hbm.at[:, cols], 1, 0, PRE),
            (sk_hbm.at[:, cols], 0, PRE, SPN),
            (sv_hbm.at[:, cols], 1, PRE, SPN),
        )

    group = x // 2
    locals_ = [
        pltpu.make_async_copy(src, kv.at[0, core, which, pl.ds(at, rows)], local_sem.at[number])
        for number, (src, which, at, rows) in enumerate(own_parts(tp * 2 + group))
    ]
    q_cols = pl.ds(pl.multiple_of(group * 2048, 2048), 2048)
    other_cols = pl.ds(pl.multiple_of((1 - group) * 2048, 2048), 2048)
    locals_.append(pltpu.make_async_copy(q_hbm.at[:, q_cols], q_raw.at[0], local_sem.at[4]))
    for copy in locals_:
        copy.start()

    pl.semaphore_wait(barrier, 8)

    swap = pltpu.make_async_remote_copy(
        src_ref=q_hbm.at[:, other_cols], dst_ref=q_raw.at[1], send_sem=q_send, recv_sem=q_recv,
        device_id=swap_device, device_id_type=MESH,
    )
    swap.start()
    sends = []
    for number, (dx, dt) in enumerate(SOURCES):
        if number == 0:
            continue
        index = SOURCES.index(((4 - dx) % 4, dt))
        target_x = lax.rem(x + dx, 4)
        head = lax.rem(tp + dt, 2) * 2 + target_x // 2
        for part, (src, which, at, rows) in enumerate(own_parts(head)):
            copy = pltpu.make_async_remote_copy(
                src_ref=src, dst_ref=kv.at[index, core, which, pl.ds(at, rows)],
                send_sem=send_sem.at[number, part], recv_sem=recv_sem.at[index],
                device_id=device(dx, dt), device_id_type=MESH,
            )
            copy.start()
            sends.append(copy)

    def forward_copy(slot):
        return pltpu.make_async_remote_copy(
            src_ref=kv.at[slot, core], dst_ref=kv.at[slot, core], send_sem=fwd_send.at[slot],
            recv_sem=fwd_recv.at[slot], device_id=sibling, device_id_type=MESH,
        )

    def arrived_sibling(slot):
        pltpu.make_async_remote_copy(
            src_ref=kv.at[slot, 1 - core], dst_ref=kv.at[slot, 1 - core], send_sem=fwd_send.at[slot],
            recv_sem=fwd_recv.at[slot], device_id=sibling, device_id_type=MESH,
        ).wait_recv()

    def forward(slot):
        pltpu.make_async_copy(kv.at[slot, core], kv.at[slot, core], recv_sem.at[slot]).wait()
        forward_copy(slot).start()

    def source(slot):
        dx = pick(slot, [s[0] for s in SOURCES])
        dt = pick(slot, [s[1] for s in SOURCES])
        return lax.rem(x + dx, 4), lax.rem(tp + dt, 2)

    def prepare(slot):
        arrived_sibling(slot)
        from_x, from_tp = source(slot)
        for c in range(2):
            keys = kv[slot, c, 0, :PRE]
            at = pl.ds(c * PRE, PRE)
            k_two[slot, at, :HD] = keys
            k_two[slot, at, HD:] = keys
            for page in range(PRE // BLK):
                v_t[slot, :HD, pl.ds(c * PRE + page * BLK, BLK)] = (
                    kv[slot, c, 1, pl.ds(page * BLK, BLK)].astype(jnp.float32).T.astype(jnp.bfloat16)
                )
            place = pl.ds(pl.multiple_of(((from_x * 2 + c) * 2 + from_tp) * SPN, SPN), SPN)
            span_keys = kv[slot, c, 0, PRE:]
            ks_two[place, :HD] = span_keys
            ks_two[place, HD:] = span_keys
            vs_raw[place] = kv[slot, c, 1, PRE:]

    def turn_queries(chunk):
        scale = math.log2(math.e) / math.sqrt(HD)

        @pl.loop(0, 16)
        def _(head):
            cols = pl.ds(pl.multiple_of(head * HD, HD), HD)
            turned = (q_raw[chunk, :, cols].astype(jnp.float32) * scale).T
            high = turned.astype(jnp.bfloat16)
            at = pl.ds(pl.multiple_of(chunk * 2048 + head * HD, HD), HD)
            q_t[:HD, at] = high
            q_t[HD:, at] = (turned - high.astype(jnp.float32)).astype(jnp.bfloat16)

    ones = jnp.ones((VR - HD, SLOT), jnp.bfloat16)
    for slot in range(8):
        v_t[slot, HD:] = ones
    vs_t[HD:] = jnp.ones((VR - HD, SPAN), jnp.bfloat16)
    key_at = lax.broadcasted_iota(jnp.int32, (BLK, QB), 0)
    row_at = lax.rem(lax.broadcasted_iota(jnp.int32, (BLK, QB), 1), BLK)
    tri[...] = jnp.where(key_at <= row_at, 0.0, LOW)
    row_max[...] = jnp.full(row_max.shape, LOW, jnp.float32)

    @pl.loop(0, 4)
    def _(q):
        acc[q] = jnp.zeros((VR, QB), jnp.float32)

    for copy in locals_[:4]:
        copy.wait()
    forward_copy(0).start()
    locals_[4].wait()
    turn_queries(0)
    prepare(0)
    forward(1)

    limit = limit_ref[0] * 8

    def visible(slot, page):
        from_x, from_tp = source(slot)
        c, inner = divmod(page, PRE // BLK)
        number = ((from_x * 2 + c) * 2 + from_tp) * (PRE // BLK) + inner
        return slot_ref[number] < limit

    def score(slot, q, buffer):
        cols = pl.ds(pl.multiple_of(q * QB, QB), QB)
        value = jnp.dot(k_two[slot], q_t[:, cols], preferred_element_type=jnp.float32)
        scores[buffer] = value
        largest = jnp.full((1, QB), LOW, jnp.float32)
        for page in range(SLOT // BLK):
            page_max = jnp.max(value[page * BLK : (page + 1) * BLK], axis=0, keepdims=True)
            largest = jnp.maximum(largest, jnp.where(visible(slot, page), page_max, LOW))
        block_max[buffer] = largest

    def update(q, largest, weights_of, values, blocks):
        before = row_max[q]
        now = jnp.maximum(before, largest)
        row_max[q] = now
        weights = jnp.concatenate([weights_of(block, now) for block in range(blocks)], axis=0)
        added = jnp.dot(values, weights, preferred_element_type=jnp.float32)
        acc[q] = acc[q] * jnp.exp2(before - now) + added

    def process(slot, q, buffer):
        def weights_of(page, now):
            shift = jnp.where(visible(slot, page), now, -LOW)
            return jnp.exp2(scores[buffer, page * BLK : (page + 1) * BLK] - shift).astype(jnp.bfloat16)

        update(q, block_max[buffer], weights_of, v_t[slot], SLOT // BLK)

    def span_step(q, ctx_of):
        cols = pl.ds(pl.multiple_of(q * QB, QB), QB)
        value = jnp.dot(ks_two[...], q_t[:, cols], preferred_element_type=jnp.float32)
        span_scores[...] = value
        mine = pl.ds(pl.multiple_of(ctx_of * BLK, BLK), BLK)
        span_scores[mine] = span_scores[mine] + tri[...]
        largest = jnp.full((1, QB), LOW, jnp.float32)
        for block in range(SPAN // BLK):
            top = jnp.max(span_scores[pl.ds(block * BLK, BLK)], axis=0, keepdims=True)
            largest = jnp.maximum(largest, jnp.where(block <= ctx_of, top, LOW))

        def weights_of(block, now):
            shift = jnp.where(block <= ctx_of, now, -LOW)
            return jnp.exp2(span_scores[pl.ds(block * BLK, BLK)] - shift).astype(jnp.bfloat16)

        update(q, largest, weights_of, vs_t[...], SPAN // BLK)

    def finish(chunk, half):
        q = chunk * 2 + half
        share = 1.0 / acc[q, HD : HD + 1]
        for head in range(8):
            at = slice(head * HD, (head + 1) * HD)
            block = acc[q, :HD, at] * share[:, at]
            heads_ref[chunk, :, pl.ds(half * QB + head * HD, HD)] = block.T.astype(jnp.bfloat16)

    first = group
    own_ctx = x * 2 + core
    swap_ctx = swap_x * 2 + core

    def chunk_of(phase):
        return jnp.where(phase == 0, 0, jnp.where(phase == 1, 1, jnp.where(phase == 2, first, 1 - first)))

    def slot_of(step):
        return lax.rem(step, 4) + 4 * (step // 8)

    score(0, 0, 0)

    @pl.loop(0, 16)
    def _(step):
        phase = step // 4
        slot = slot_of(step)
        chunk = chunk_of(phase)
        later = jnp.minimum(step + 1, 15)

        @pl.when(step < 2)
        def _():
            forward(step + 2)

        @pl.when((step >= 4) & (step < 8))
        def _():
            forward(step)

        @pl.when((step < 3) | ((step >= 7) & (step < 11)))
        def _():
            prepare(slot_of(later))

        @pl.when(step == 3)
        def _():
            swap.wait_recv()
            turn_queries(1)

        score(slot, chunk * 2 + 1, 1)
        process(slot, chunk * 2, 0)
        score(slot_of(later), chunk_of(later // 4) * 2, 0)
        process(slot, chunk * 2 + 1, 1)

        @pl.when(step == 11)
        def _():
            for block in range(SPAN // BLK):
                at = pl.ds(block * BLK, BLK)
                vs_t[:HD, at] = vs_raw[at].astype(jnp.float32).T.astype(jnp.bfloat16)

        @pl.when((step == 11) | (step == 15))
        def _():
            @pl.loop(0, 2)
            def _(half):
                span_step(chunk * 2 + half, jnp.where(chunk == 0, own_ctx, swap_ctx))

            for half in range(2):
                finish(chunk, half)

    for copy in sends:
        copy.wait_send()
    swap.wait_send()

    @pl.loop(0, 8)
    def _(slot):
        forward_copy(slot).wait_send()


def attention(queries, span_keys, span_values, prefix_keys, prefix_values, block_slot, span_index):
    any_spec = pl.BlockSpec(memory_space=pl.ANY)
    smem = pl.BlockSpec(memory_space=pltpu.SMEM)
    vmem = pl.BlockSpec(memory_space=pltpu.VMEM)
    dma = pltpu.SemaphoreType.DMA
    bf16, f32 = jnp.bfloat16, jnp.float32
    return pl.pallas_call(
        attention_kernel,
        out_shape=jax.ShapeDtypeStruct((2, BLK, 2048), bf16),
        in_specs=[any_spec] * 5 + [smem, smem],
        out_specs=vmem,
        scratch_shapes=[
            pltpu.VMEM((8, 2, 2, PRE + SPN, HD), bf16),
            pltpu.VMEM((2, BLK, 2048), bf16),
            pltpu.VMEM((2 * HD, 4 * QB), bf16),
            pltpu.VMEM((8, SLOT, 2 * HD), bf16),
            pltpu.VMEM((8, VR, SLOT), bf16),
            pltpu.VMEM((SPAN, 2 * HD), bf16),
            pltpu.VMEM((SPAN, HD), bf16),
            pltpu.VMEM((VR, SPAN), bf16),
            pltpu.VMEM((2, SLOT, QB), f32),
            pltpu.VMEM((SPAN, QB), f32),
            pltpu.VMEM((BLK, QB), f32),
            pltpu.VMEM((2, 1, QB), f32),
            pltpu.VMEM((4, 1, QB), f32),
            pltpu.VMEM((4, VR, QB), f32),
            dma((8, 4)), dma((8,)), dma((8,)), dma((8,)), dma(()), dma(()), dma((5,)),
        ],
        compiler_params=pltpu.CompilerParams(
            collective_id=0, has_side_effects=True, vmem_limit_bytes=56 << 20
        ),
        name="attention",
    )(queries, span_keys, span_values, prefix_keys, prefix_values, block_slot, span_index)


def per_device(
    queries, span_keys, span_values, prefix_keys, prefix_values, out_weight, residual, block_slot, span_index
):
    heads = attention(
        queries[0], span_keys[0], span_values[0], prefix_keys[0], prefix_values[0], block_slot, span_index
    )
    every = lax.all_gather(heads, "ctx", axis=0)
    rows = []
    for ctx in range(8):
        other = (3 - ctx // 2) * 2 + ctx % 2
        pair = (every[ctx, 0], every[other, 1])
        rows.append(jnp.concatenate(pair if ctx < 4 else pair[::-1], axis=1))
    partial = jnp.dot(jnp.concatenate(rows, axis=0), out_weight[0], preferred_element_type=jnp.float32)
    summed = lax.psum_scatter(partial.astype(jnp.bfloat16), "tp", scatter_dimension=0, tiled=True)
    layer = (residual[0].astype(jnp.float32) + summed.astype(jnp.float32)).astype(jnp.bfloat16)
    sections = lax.axis_size("section")
    return lax.ppermute(layer, "section", [(i, (i + 1) % sections) for i in range(sections)])[None]


def solution(mesh):
    in_specs = (
        P("section", "ctx", "tp"),
        P("section", ("ctx", "tp"), None),
        P("section", ("ctx", "tp"), None),
        P("section", ("ctx", "tp"), None),
        P("section", ("ctx", "tp"), None),
        P("section", "tp", "ctx"),
        P("section", "tp", "ctx"),
        P(),
        P("section"),
    )
    return jax.shard_map(
        per_device, mesh=mesh, in_specs=in_specs, out_specs=P("section", "tp", "ctx"), check_vma=False
    )
```

time: 912 us -> 225 us (0.25)
  matrix products: 293 us -> 10.1 us
  local copies, waits for them, and re-layouts: 204 us -> 7.55 us
  waiting for transfers between devices: 249 us -> 113 us
  other arithmetic: 90 us -> 2.34 us
  Pallas kernels: 0 us -> 77.6 us
  loops' own time: 54.5 us -> 0 us
    dot_general x129 -> x1, matrix products: 293 us -> 10.1 us  [per_device(): jnp.dot(jnp.concatenate(rows, axis=0), out_weight[0], preferred_element_t...]
    dynamic_slice x226 -> x0, local copies, waits for them, and re-layouts: 161 us -> none  [the longest x192 113 us: per_shard(): lax.scan(per_page, shard_state, (page_keys, page_values, page_slots))]
    all_gather x3 -> x1, waiting for transfers between devices: 186 us -> 51 us  [per_device(): every = lax.all_gather(heads, 'ctx', axis=0)]
    pallas_call x0 -> x1, Pallas kernels: none -> 77.6 us  [attention(): pl.pallas_call(attention_kernel, out_shape=jax.ShapeDtypeStruct((2, BLK,...]
    another operation x17 -> x0, loops' own time: 54.5 us -> none  [the longest x16 32.4 us: per_shard(): lax.scan(per_page, shard_state, (page_keys, page_values, page_slots))]
    while x32 -> x0, other arithmetic: 49.5 us -> none
    slice x32 -> x0, local copies, waits for them, and re-layouts: 40.2 us -> none  [the longest x16 27.6 us: per_shard(): page_values = shard_values[:prefix_rows].reshape(pages_per, BLK, columns)]
    reduce_sum x64 -> x0, other arithmetic: 29.5 us -> none  [attend(): running_sum = running_sum * rescale + jnp.sum(weights, axis=2)]
  transfers between devices with their start and end apart: 5 -> 3, of which waited for: 5 -> 3; matrix products, arithmetic and copies ran while one was open for 1% -> 0% of each run, Pallas kernels for 0% -> 0%
where the time goes in v1:
time: 225 us
  waiting for transfers between devices  113 us (50%)
  Pallas kernels  77.6 us (34%)
  between operations  14.2 us (6%)
  matrix products  10.1 us (4%)
  local copies, waits for them, and re-layouts  7.55 us (3%)
  other arithmetic  2.34 us (1%)
    pallas_call x1, Pallas kernels, attention(): pl.pallas_call(attention_kernel, out_shape=jax.ShapeDtypeStruct((2, BLK,...  77.6 us
    all_gather x1, waiting for transfers between devices, per_device(): every = lax.all_gather(heads, 'ctx', axis=0)  51 us
    reduce_scatter x1, waiting for transfers between devices, per_device(): lax.psum_scatter(partial.astype(jnp.bfloat16), 'tp', scatter_dimension=0,...  35.8 us
    ppermute x1, waiting for transfers between devices, per_device(): lax.ppermute(layer, 'section', [(i, (i + 1) % sections) for i in range(se...  25.8 us
    dot_general x1, matrix products, per_device(): jnp.dot(jnp.concatenate(rows, axis=0), out_weight[0], preferred_element_t...  10.1 us
  transfers between devices with their start and end apart: 3, of which 3 were waited for; matrix products, arithmetic and copies ran while one was open for 0% of the time, Pallas kernels for 0%

profile of v1, /device:TPU:1, one launch (start us, length us, event | category | flops | bytes accessed | tf_op | source)
XLA Modules:
  0.0 224.9 jit_solution(7433966709639965869)
XLA Ops:
  7.2 77.6 %attention.1 = bf16[2,128,2048]{2,1,0:T(8,128)(2,1)} custom-call(bf16[128,4096]{1,0:T(8,128)(2,1)} %bitcast.49, bf16[64,512]{1,0:T(8,128)(2,1)} %bitcast.53, bf16[64,512]{1,0:T(8,128)(2,1)} %bitcast.54, bf16[384,512]{1,0:T(8,128)(2,1)} %bitcast.51, bf16[384,512]{1,0:T(8,128)(2,1)} %bitcast.52, s32[48]{0:T(128)} %slot_ref.1, s32[1]{0:T(128)S(6)} %copy.18.limit_ref), custom_call_target="tpu_custom_call" | custom-call | tf_op jit(solution)/shard_map/attention/pallas_call | solution.py:299
  84.8 0.0 all-gather.3.cloned.1.call-update
  84.9 0.0 reduce-scatter.2.cloned.1.call-start
  84.9 51.0 %all-gather.3.cloned.1.call-done = bf16[16,128,2048]{2,1,0:T(8,128)(2,1)} async-done(((bf16[2,128,2048]{2,1,0:T(8,128)(2,1)}), bf16[16,128,2048]{2,1,0:T(8,128)(2,1)}) %all-gather.3.cloned.1.call-update) | async-done | bytes 8388624 | tf_op jit(solution)/shard_map/all_gather | solution.py:334
  135.9 3.8 %slice_bitcast_fusion.1 = (bf16[128,2048]{1,0:T(8,128)(2,1)S(1)}, bf16[128,2048]{1,0:T(8,128)(2,1)S(1)}, bf16[128,2048]{1,0:T(8,128)(2,1)S(1)}, bf16[128,2048]{1...) fusion(bf16[8,2,128,2048]{3,2,1,0:T(8,128)(2,1)} %bitcast.48), kind=kLoop, calls=%fused_computation.14 | loop fusion | bytes 16777216 | tf_op jit(solution)/shard_map/squeeze | solution.py:338
  139.7 0.0 slice-start
  139.7 0.1 maximum_dynamic-update-slice_fusion.7
  139.8 0.1 maximum_dynamic-update-slice_fusion.6
  139.9 0.1 maximum_dynamic-update-slice_fusion.5
  140.0 0.1 maximum_dynamic-update-slice_fusion.4
  140.1 0.0 slice-start.1
  140.1 0.1 maximum_dynamic-update-slice_fusion.3
  140.2 0.1 maximum_dynamic-update-slice_fusion.2
  140.3 0.1 maximum_dynamic-update-slice_fusion.1
  140.4 0.1 maximum_dynamic-update-slice_fusion
  140.5 1.4 slice-done
  141.9 1.4 slice-done.1
  143.3 10.1 %fusion.3 = bf16[1024,1024]{1,0:T(8,128)(2,1)} fusion(bf16[1024,4096]{1,0:T(8,128)(2,1)S(1)} %maximum_dynamic-update-slice_fusion, bf16[1,4096,1024]{2,1,0:T(8,128)(2,1)S(1)} %bitcast.56), kind=kOutput, calls=%fused_computation.4 | convolution fusion | flops 8590983168 | bytes 18874368 | tf_op jit(solution)/shard_map/dot_general | solution.py:340
  153.4 0.0 reduce-scatter.2.cloned.1.call-update
  153.4 35.8 %reduce-scatter.2.cloned.1.call-done = bf16[512,1024]{1,0:T(8,128)(2,1)} async-done(((bf16[1024,1024]{1,0:T(8,128)(2,1)}), bf16[512,1024]{1,0:T(8,128)(2,1)}) %reduce-scatter.2.cloned.1.call-update) | async-done | bytes 1048592 | tf_op jit(solution)/shard_map/reduce_scatter | solution.py:341
  189.2 1.6 fusion.2
  190.8 0.4 collective-permute-start
  191.2 25.8 %collective-permute-done = bf16[512,1024]{1,0:T(8,128)(2,1)S(1)} collective-permute-done((bf16[512,1024]{1,0:T(8,128)(2,1)S(1)}, bf16[512,1024]{1,0:T(8,128)(2,1)S(1)}, u32[]{:S(2)}, u32[]{:S(2)}) %collective-permute-start) | collective-permute-done | bytes 1048608 | tf_op jit(solution)/shard_map/ppermute | solution.py:344
  217.0 1.0 copy.19
  (4 shorter events, 0.0 us)
Async XLA Ops:
  6.5 129.4 %all-gather.3.cloned.1.call-start = ((), (), s32[]{:S(2)}) async-start(), calls=%async_computation.2 | async-start | bytes 9437184 | tf_op jit(solution)/shard_map/all_gather | solution.py:334
  84.9 104.3 %reduce-scatter.2.cloned.1.call-start = ((), (), s32[]{:S(2)}) async-start(), calls=%async_computation.1 | async-start | bytes 3145728 | tf_op jit(solution)/shard_map/reduce_scatter | solution.py:341
  139.7 2.2 slice-start
  140.1 3.2 %slice-start.1 = ((s8[8388608]{0:T(1024)(128)(4,1)}), s8[4194304]{0:T(1024)(128)(4,1)S(1)}, s32[]{:S(2)}) async-start(s8[8388608]{0:T(1024)(128)(4,1)} %bitcast.55), calls=%async_computation.4 | async-start | bytes 8388608
  143.3 45.9 %copy-start = (bf16[1,512,1024]{2,1,0:T(8,128)(2,1)S(1)}, bf16[1,512,1024]{2,1,0:T(8,128)(2,1)}, u32[]{:S(2)}) copy-start(bf16[1,512,1024]{2,1,0:T(8,128)(2,1)} %param.15) | copy-start | bytes 3145732
  190.8 26.2 %collective-permute-start = (bf16[512,1024]{1,0:T(8,128)(2,1)S(1)}, bf16[512,1024]{1,0:T(8,128)(2,1)S(1)}, u32[]{:S(2)}, u32[]{:S(2)}) collective-permute-start(bf16[512,1024]{1,0:T(8,128)(2,1)S(1)} %fusion.2), channel_id=1, source_target_pairs={{0,16},{16,32},{32,48},{48,64},{64,80},{80,96},{96,112},{112,0},{1... | collective-permute-start | bytes 3145736 | tf_op jit(solution)/shard_map/ppermute | solution.py:344
Sparse Core Ops, SparseCore 0:
  85.0 50.8 all-gather.2
  153.5 35.6 reduce-scatter.1

commit v2 on v1

--- a/solution.py
+++ b/solution.py
@@ -18,6 +18,8 @@
 SPAN = 1024
 VR = 144
 LOW = -1e30
+FIRST_ROWS = (0, 2, 2, 0)
+LAST_ROWS = (3, 1, 1, 3)
 SOURCES = ((0, 0), (1, 0), (3, 0), (0, 1), (1, 1), (3, 1), (2, 0), (2, 1))
 
 
@@ -33,10 +35,10 @@
     return value
 
 
-def attention_kernel(
-    q_hbm, sk_hbm, sv_hbm, pk_hbm, pv_hbm, slot_ref, limit_ref, heads_ref,
-    kv, q_raw, q_t, k_two, v_t, ks_two, vs_raw, vs_t, scores, span_scores, tri, block_max, row_max, acc,
-    send_sem, recv_sem, fwd_send, fwd_recv, q_send, q_recv, local_sem,
+def layer_kernel(
+    q_hbm, sk_hbm, sv_hbm, pk_hbm, pv_hbm, w_hbm, res_hbm, slot_ref, limit_ref, out_ref,
+    heads, weight, rest, total, part, got, kv, q_raw, q_t, k_two, v_t, ks_two, vs_raw, vs_t, scores, span_scores, tri, block_max, row_max, acc,
+    send_sem, recv_sem, fwd_send, fwd_recv, q_send, q_recv, local_sem, g_send, g_recv, h_send, h_recv,
 ):
     section, x, core, tp = where_am_i()
     swap_x = 3 - x
@@ -47,10 +49,14 @@
     sibling = (section, x * 2 + 1 - core, tp)
     swap_device = (section, swap_x * 2 + core, tp)
 
+    next_section, last_section = lax.rem(section + 1, 8), lax.rem(section + 7, 8)
+    ctx = x * 2 + core
     barrier = pltpu.get_barrier_semaphore()
     for dx, dt in SOURCES[1:]:
         pl.semaphore_signal(barrier, inc=1, device_id=device(dx, dt), device_id_type=MESH)
     pl.semaphore_signal(barrier, inc=1, device_id=sibling, device_id_type=MESH)
+    for half in range(2):
+        pl.semaphore_signal(barrier, inc=1, device_id=(last_section, ctx, half), device_id_type=MESH)
 
     def own_parts(head):
         cols = pl.ds(pl.multiple_of(head * HD, HD), HD)
@@ -69,10 +75,12 @@
     q_cols = pl.ds(pl.multiple_of(group * 2048, 2048), 2048)
     other_cols = pl.ds(pl.multiple_of((1 - group) * 2048, 2048), 2048)
     locals_.append(pltpu.make_async_copy(q_hbm.at[:, q_cols], q_raw.at[0], local_sem.at[4]))
+    locals_.append(pltpu.make_async_copy(w_hbm, weight, local_sem.at[5]))
+    locals_.append(pltpu.make_async_copy(res_hbm, rest, local_sem.at[6]))
     for copy in locals_:
         copy.start()
 
-    pl.semaphore_wait(barrier, 8)
+    pl.semaphore_wait(barrier, 10)
 
     swap = pltpu.make_async_remote_copy(
         src_ref=q_hbm.at[:, other_cols], dst_ref=q_raw.at[1], send_sem=q_send, recv_sem=q_recv,
@@ -86,10 +94,10 @@
         index = SOURCES.index(((4 - dx) % 4, dt))
         target_x = lax.rem(x + dx, 4)
         head = lax.rem(tp + dt, 2) * 2 + target_x // 2
-        for part, (src, which, at, rows) in enumerate(own_parts(head)):
+        for piece, (src, which, at, rows) in enumerate(own_parts(head)):
             copy = pltpu.make_async_remote_copy(
                 src_ref=src, dst_ref=kv.at[index, core, which, pl.ds(at, rows)],
-                send_sem=send_sem.at[number, part], recv_sem=recv_sem.at[index],
+                send_sem=send_sem.at[number, piece], recv_sem=recv_sem.at[index],
                 device_id=device(dx, dt), device_id_type=MESH,
             )
             copy.start()
@@ -217,15 +225,100 @@
 
         update(q, largest, weights_of, vs_t[...], SPAN // BLK)
 
-    def finish(chunk, half):
+    def rows_of(chip, turn):
+        return jnp.where(turn == 0, pick(chip, FIRST_ROWS), pick(chip, LAST_ROWS))
+
+    def place(dx, turn, half, c):
+        chip = lax.rem(x + dx, 4)
+        return heads.at[rows_of(chip, turn), chip // 2, half, c]
+
+    right, left = device(1, 0), device(3, 0)
+
+    def moved(kind, turn, half):
+        top, bottom = pl.ds(0, BLK // 2), pl.ds(BLK // 2, BLK // 2)
+        if kind == 0:
+            src, to, dst = place(0, turn, half, core), right, place(3, turn, half, core)
+        elif kind == 1:
+            src, to, dst = place(0, turn, half, core), left, place(1, turn, half, core)
+        elif kind == 2:
+            src, to, dst = place(3, turn, half, core).at[top], right, place(2, turn, half, core).at[top]
+        elif kind == 3:
+            src, to, dst = place(1, turn, half, core).at[bottom], left, place(2, turn, half, core).at[bottom]
+        else:
+            dx = (0, 3, 1, 2)[kind - 4]
+            src, to, dst = place(dx, turn, half, core), sibling, place(dx, turn, half, 1 - core)
+        piece = turn * 2 + half
+        sems = (g_send.at[piece, kind], g_recv.at[piece, kind])
+        make = functools.partial(
+            pltpu.make_async_remote_copy, send_sem=sems[0], recv_sem=sems[1], device_id=to, device_id_type=MESH
+        )
+        return make(src_ref=src, dst_ref=src), make(src_ref=dst, dst_ref=dst)
+
+    def send(kind, turn, half):
+        moved(kind, turn, half)[0].start()
+
+    def arrived(kind, turn, half):
+        moved(kind, turn, half)[1].wait_recv()
+
+    def finish(chunk, half, turn):
         q = chunk * 2 + half
         share = 1.0 / acc[q, HD : HD + 1]
+        mine = place(0, turn, half, core)
         for head in range(8):
             at = slice(head * HD, (head + 1) * HD)
             block = acc[q, :HD, at] * share[:, at]
-            heads_ref[chunk, :, pl.ds(half * QB + head * HD, HD)] = block.T.astype(jnp.bfloat16)
-
-    first = group
+            mine[:, pl.ds(head * HD, HD)] = block.T.astype(jnp.bfloat16)
+        for kind in (0, 1, 4):
+            send(kind, turn, half)
+
+    def pass_on(turn, half):
+        arrived(0, turn, half)
+        send(2, turn, half)
+        send(5, turn, half)
+        arrived(1, turn, half)
+        send(3, turn, half)
+        send(6, turn, half)
+
+    def pass_far(turn, half):
+        arrived(2, turn, half)
+        arrived(3, turn, half)
+        send(7, turn, half)
+
+    def project(rows, kv_head, second):
+        tile = 256
+        half_at = rows // 2
+        inside = pl.ds(pl.multiple_of(lax.rem(rows, 2) * 256, 256), 256)
+
+        @pl.loop(0, 1024 // tile)
+        def _(number):
+            cols = pl.ds(pl.multiple_of(number * tile, tile), tile)
+            value = jnp.zeros((256, tile), jnp.float32)
+            for half in range(2):
+                depth = pl.ds(pl.multiple_of(kv_head * 2048 + half * 1024, 1024), 1024)
+                value += jnp.dot(
+                    heads[rows, kv_head, half].reshape(256, 1024), weight[depth, cols],
+                    preferred_element_type=jnp.float32,
+                )
+            if second:
+                extra = jnp.where(half_at == tp, rest[inside, cols].astype(jnp.float32), 0.0)
+                part[rows, :, cols] = (total[:, cols] + value + extra).astype(jnp.bfloat16)
+            else:
+                total[:, cols] = value
+
+    def hand_on(rows):
+        return pltpu.make_async_remote_copy(
+            src_ref=part.at[rows], dst_ref=got.at[tp, lax.rem(rows, 2)], send_sem=h_send.at[rows],
+            recv_sem=h_recv.at[tp, lax.rem(rows, 2)], device_id=(next_section, ctx, rows // 2), device_id_type=MESH,
+        )
+
+    def handed(from_tp, turn):
+        ref = got.at[from_tp, turn]
+        pltpu.make_async_remote_copy(
+            src_ref=ref, dst_ref=ref, send_sem=h_send.at[turn], recv_sem=h_recv.at[from_tp, turn],
+            device_id=sibling, device_id_type=MESH,
+        ).wait_recv()
+
+    first = lax.rem(x, 2)
     own_ctx = x * 2 + core
     swap_ctx = swap_x * 2 + core
 
@@ -277,9 +370,57 @@
             @pl.loop(0, 2)
             def _(half):
                 span_step(chunk * 2 + half, jnp.where(chunk == 0, own_ctx, swap_ctx))
-
+                finish(chunk, half, phase - 2)
+
+        @pl.when(step >= 14)
+        def _():
+            pass_on(0, step - 14)
+
+    locals_[5].wait()
+    locals_[6].wait()
+    near = jnp.where(first == 0, x + 1, x - 1)
+
+    @pl.loop(0, 2)
+    def _(turn):
+        mine, other = rows_of(x, turn), rows_of(near, turn)
+
+        @pl.when(turn == 1)
+        def _():
             for half in range(2):
-                finish(chunk, half)
+                pass_on(turn, half)
+
+        for half in range(2):
+            arrived(4, turn, half)
+        project(mine, group, False)
+        for half in range(2):
+            arrived(5, turn, half)
+            arrived(6, turn, half)
+        project(mine, 1 - group, True)
+        hand_on(mine).start()
+        for half in range(2):
+            pass_far(turn, half)
+        project(other, group, False)
+        for half in range(2):
+            arrived(7, turn, half)
+        project(other, 1 - group, True)
+        hand_on(other).start()
+
+    @pl.loop(0, 2)
+    def _(turn):
+        for from_tp in range(2):
+            handed(from_tp, turn)
+        at = pl.ds(pl.multiple_of(turn * 256, 256), 256)
+        out_ref[at] = (got[0, turn].astype(jnp.float32) + got[1, turn].astype(jnp.float32)).astype(jnp.bfloat16)
+
+    @pl.loop(0, 2)
+    def _(turn):
+        for half in range(2):
+            for kind in range(8):
+                moved(kind, turn, half)[0].wait_send()
+
+    @pl.loop(0, 4)
+    def _(rows):
+        hand_on(rows).wait_send()
 
     for copy in sends:
         copy.wait_send()
@@ -290,18 +431,26 @@
         forward_copy(slot).wait_send()
 
 
-def attention(queries, span_keys, span_values, prefix_keys, prefix_values, block_slot, span_index):
+def layer(
+    queries, span_keys, span_values, prefix_keys, prefix_values, out_weight, residual, block_slot, span_index
+):
     any_spec = pl.BlockSpec(memory_space=pl.ANY)
     smem = pl.BlockSpec(memory_space=pltpu.SMEM)
     vmem = pl.BlockSpec(memory_space=pltpu.VMEM)
     dma = pltpu.SemaphoreType.DMA
     bf16, f32 = jnp.bfloat16, jnp.float32
     return pl.pallas_call(
-        attention_kernel,
-        out_shape=jax.ShapeDtypeStruct((2, BLK, 2048), bf16),
-        in_specs=[any_spec] * 5 + [smem, smem],
+        layer_kernel,
+        out_shape=jax.ShapeDtypeStruct((512, 1024), bf16),
+        in_specs=[any_spec] * 7 + [smem, smem],
         out_specs=vmem,
         scratch_shapes=[
+            pltpu.VMEM((4, 2, 2, 2, BLK, 1024), bf16),
+            pltpu.VMEM((4096, 1024), bf16),
+            pltpu.VMEM((512, 1024), bf16),
+            pltpu.VMEM((256, 1024), f32),
+            pltpu.VMEM((4, 256, 1024), bf16),
+            pltpu.VMEM((2, 2, 256, 1024), bf16),
             pltpu.VMEM((8, 2, 2, PRE + SPN, HD), bf16),
             pltpu.VMEM((2, BLK, 2048), bf16),
             pltpu.VMEM((2 * HD, 4 * QB), bf16),
@@ -316,32 +465,25 @@
             pltpu.VMEM((2, 1, QB), f32),
             pltpu.VMEM((4, 1, QB), f32),
             pltpu.VMEM((4, VR, QB), f32),
-            dma((8, 4)), dma((8,)), dma((8,)), dma((8,)), dma(()), dma(()), dma((5,)),
+            dma((8, 4)), dma((8,)), dma((8,)), dma((8,)), dma(()), dma(()), dma((7,)),
+            dma((4, 8)), dma((4, 8)), dma((4,)), dma((2, 2)),
         ],
         compiler_params=pltpu.CompilerParams(
-            collective_id=0, has_side_effects=True, vmem_limit_bytes=56 << 20
+            collective_id=0, has_side_effects=True, vmem_limit_bytes=60 << 20
         ),
-        name="attention",
-    )(queries, span_keys, span_values, prefix_keys, prefix_values, block_slot, span_index)
+        name="layer",
+    )(
+        queries, span_keys, span_values, prefix_keys, prefix_values, out_weight, residual, block_slot, span_index
+    )
 
 
 def per_device(
     queries, span_keys, span_values, prefix_keys, prefix_values, out_weight, residual, block_slot, span_index
 ):
-    heads = attention(
-        queries[0], span_keys[0], span_values[0], prefix_keys[0], prefix_values[0], block_slot, span_index
-    )
-    every = lax.all_gather(heads, "ctx", axis=0)
-    rows = []
-    for ctx in range(8):
-        other = (3 - ctx // 2) * 2 + ctx % 2
-        pair = (every[ctx, 0], every[other, 1])
-        rows.append(jnp.concatenate(pair if ctx < 4 else pair[::-1], axis=1))
-    partial = jnp.dot(jnp.concatenate(rows, axis=0), out_weight[0], preferred_element_type=jnp.float32)
-    summed = lax.psum_scatter(partial.astype(jnp.bfloat16), "tp", scatter_dimension=0, tiled=True)
-    layer = (residual[0].astype(jnp.float32) + summed.astype(jnp.float32)).astype(jnp.bfloat16)
-    sections = lax.axis_size("section")
-    return lax.ppermute(layer, "section", [(i, (i + 1) % sections) for i in range(sections)])[None]
+    return layer(
+        queries[0], span_keys[0], span_values[0], prefix_keys[0], prefix_values[0], out_weight[0], residual[0],
+        block_slot, span_index,
+    )[None]
 
 
 def solution(mesh):

time: 225 us -> 153 us (0.68)
  the two profiles are of different devices: /device:TPU:1 before, /device:TPU:16 now
where the time goes in v2:
time: 153 us
  Pallas kernels  150 us (98%)
  local copies, waits for them, and re-layouts  2.26 us (1%)
    pallas_call x1, Pallas kernels, layer(): pl.pallas_call(layer_kernel, out_shape=jax.ShapeDtypeStruct((512, 1024),...  150 us

profile of v2, /device:TPU:16, one launch (start us, length us, event | category | flops | bytes accessed | tf_op | source)
XLA Modules:
  0.0 152.9 jit_solution(11581341079908160935)
XLA Ops:
  0.7 150.0 %layer.1 = bf16[512,1024]{1,0:T(8,128)(2,1)} custom-call(bf16[128,4096]{1,0:T(8,128)(2,1)} %bitcast.10, bf16[64,512]{1,0:T(8,128)(2,1)} %bitcast.14, bf16[64,512]{1,0:T(8,128)(2,1)} %bitcast.15, bf16[384,512]{1,0:T(8,128)(2,1)} %bitcast.12, bf16[384,512]{1,0:T(8,128)(2,1)} %bitcast.13, bf16[4096,1024]{1,0:T(8,128)(2,1)} %bitcast.8, ...), custom_call_target="tpu_custom_call" | custom-call | tf_op jit(solution)/shard_map/layer/pallas_call | solution.py:442
  150.6 2.3 %copy.12 = bf16[1,512,1024]{2,1,0:T(8,128)(2,1)} copy(bf16[1,512,1024]{2,1,0:T(8,128)(2,1)} %bitcast.9) | data formatting | bytes 2097152

commit v3 on v1

v3 whole, which is shorter than its diff:
```python
import functools
import math

import jax
import jax.numpy as jnp
from jax import lax
from jax.experimental import pallas as pl
from jax.experimental.pallas import tpu as pltpu
from jax.sharding import PartitionSpec as P

MESH = pl.DeviceIdType.MESH
HD = 128
BLK = 128
HALF = 64
QB = 1024
PRE = 384
SPN = 64
ROWS = PRE + SPN
SLOT = 2 * ROWS
VR = 144
LOW = -1e30
SLOTS = ((0, 0), (0, 1), (1, 0), (2, 0), (1, 1), (2, 1), (3, 0), (3, 1))


def pick(index, table):
    value = jnp.int32(table[-1])
    for position in range(len(table) - 1):
        value = jnp.where(index == position, jnp.int32(table[position]), value)
    return value


def aligned(start, size):
    return pl.ds(pl.multiple_of(start, size), size)


def layer_kernel(
    q_hbm, sk_hbm, sv_hbm, pk_hbm, pv_hbm, w_hbm, res_hbm, slot_ref, limit_ref, out_ref,
    heads, weight, rest, total, part, got, summed, final, stage, kv, q_raw, q_t, k_two, v_t, scores, tri,
    block_max, row_max, acc,
    stage_sem, local_sem, send_sem, recv_sem, fwd_send, fwd_recv, relay_send, q_send, q_recv,
    g_send, g_recv, h_send, h_recv, z_send, z_recv,
):
    section, ctx, tp = lax.axis_index("section"), lax.axis_index("ctx"), lax.axis_index("tp")
    x, core = ctx // 2, lax.rem(ctx, 2)
    near = x + 1 - 2 * lax.rem(x, 2)
    chips = (x, near, 3 - x, 3 - near)
    group = x // 2
    odd = lax.rem(section, 2)

    def device(kind, dt=0):
        return (section, chips[kind] * 2 + core, lax.rem(tp + dt, 2))

    sibling = (section, x * 2 + 1 - core, tp)
    twin_section = section + 1 - 2 * odd
    above, below = lax.rem(section + 2, 8), lax.rem(section + 6, 8)

    barrier = pltpu.get_barrier_semaphore()
    greeted = [device(kind, dt) for kind, dt in SLOTS[1:6]] + [sibling]
    greeted += [(twin_section, ctx, half) for half in range(2)] + [(below, ctx, tp)]
    for other in greeted:
        pl.semaphore_signal(barrier, inc=1, device_id=other, device_id_type=MESH)

    def load_rows(head, dst, sem):
        cols = aligned(head * HD, HD)
        for src, which, at, rows in (
            (pk_hbm, 0, 0, PRE), (pv_hbm, 1, 0, PRE), (sk_hbm, 0, PRE, SPN), (sv_hbm, 1, PRE, SPN)
        ):
            pltpu.make_async_copy(src.at[:, cols], dst.at[which, pl.ds(at, rows)], sem).start()

    blocks = [kv.at[0, core]] + [stage.at[number] for number in range(3)]
    held = ((tp, group), (tp, 1 - group), (1 - tp, group), (1 - tp, 1 - group))
    for number, (side, which) in enumerate(held):
        load_rows(side * 2 + which, blocks[number], stage_sem.at[number])
    own_queries = pltpu.make_async_copy(q_hbm.at[:, aligned(group * 2048, 2048)], q_raw.at[0], local_sem.at[0])
    own_queries.start()

    def wait_block(number):
        pltpu.make_async_copy(blocks[number], blocks[number], stage_sem.at[number]).wait()

    swap = pltpu.make_async_remote_copy(
        src_ref=q_hbm.at[:, aligned((1 - group) * 2048, 2048)], dst_ref=q_raw.at[1], send_sem=q_send,
        recv_sem=q_recv, device_id=device(2), device_id_type=MESH,
    )

    def row_send(slot):
        kind, dt = SLOTS[slot]
        return pltpu.make_async_remote_copy(
            src_ref=blocks[2 * dt + (kind == 2)], dst_ref=kv.at[slot, core], send_sem=send_sem.at[slot],
            recv_sem=recv_sem.at[slot], device_id=device(kind, dt), device_id_type=MESH,
        )

    def relay(slot, to):
        return pltpu.make_async_remote_copy(
            src_ref=kv.at[slot, core], dst_ref=kv.at[to, core], send_sem=relay_send.at[to - 6],
            recv_sem=recv_sem.at[to], device_id=device(1), device_id_type=MESH,
        )

    def to_sibling(slot):
        return pltpu.make_async_remote_copy(
            src_ref=kv.at[slot, core], dst_ref=kv.at[slot, core], send_sem=fwd_send.at[slot],
            recv_sem=fwd_recv.at[slot], device_id=sibling, device_id_type=MESH,
        )

    def arrived_sibling(slot):
        ref = kv.at[slot, 1 - core]
        pltpu.make_async_remote_copy(
            src_ref=ref, dst_ref=ref, send_sem=fwd_send.at[slot], recv_sem=fwd_recv.at[slot],
            device_id=sibling, device_id_type=MESH,
        ).wait_recv()

    def forward(slot):
        pltpu.make_async_copy(kv.at[slot, core], kv.at[slot, core], recv_sem.at[slot]).wait()
        to_sibling(slot).start()

    for number in range(4):
        wait_block(number)
    pl.semaphore_wait(barrier, len(greeted))
    for slot in (3, 2, 1):
        row_send(slot).start()
    to_sibling(0).start()
    load_weight = pltpu.make_async_copy(w_hbm, weight, local_sem.at[1])
    load_rest = pltpu.make_async_copy(res_hbm, rest, local_sem.at[2])
    load_weight.start()
    load_rest.start()

    def source(slot):
        kind = pick(slot, [s[0] for s in SLOTS])
        dt = pick(slot, [s[1] for s in SLOTS])
        chip = jnp.where(kind == 0, x, jnp.where(kind == 1, near, jnp.where(kind == 2, 3 - x, 3 - near)))
        return chip, lax.rem(tp + dt, 2)

    def prepare(slot):
        for c in range(2):
            for start, size, at in ((0, PRE, c * PRE), (PRE, SPN, 2 * PRE + c * SPN)):
                keys = kv[slot, c, 0, pl.ds(start, size)]
                k_two[slot, pl.ds(at, size), :HD] = keys
                k_two[slot, pl.ds(at, size), HD:] = keys
            for page in range(PRE // BLK):
                v_t[slot, :HD, pl.ds(c * PRE + page * BLK, BLK)] = kv[slot, c, 1, pl.ds(page * BLK, BLK)].T
        span_values = jnp.concatenate([kv[slot, c, 1, pl.ds(PRE, SPN)] for c in range(2)], axis=0)
        v_t[slot, :HD, pl.ds(2 * PRE, BLK)] = span_values.T

    def turn_queries(chunk):
        scale = math.log2(math.e) / math.sqrt(HD)

        @pl.loop(0, 8)
        def _(pair):
            for half in range(2):
                rows = pl.ds(half * HALF, HALF)
                block = jnp.concatenate(
                    [q_raw[chunk, rows, aligned((2 * pair + one) * HD, HD)] for one in range(2)], axis=0
                )
                turned = (block.astype(jnp.float32) * scale).T
                high = turned.astype(jnp.bfloat16)
                at = aligned((chunk * 2 + half) * QB + pair * HD, HD)
                q_t[:HD, at] = high
                q_t[HD:, at] = (turned - high.astype(jnp.float32)).astype(jnp.bfloat16)

    ones = jnp.ones((VR - HD, SLOT), jnp.bfloat16)
    for slot in range(8):
        v_t[slot, HD:] = ones
    key_at = lax.broadcasted_iota(jnp.int32, (SPN, QB), 0)
    row_at = lax.rem(lax.broadcasted_iota(jnp.int32, (SPN, QB), 1), HALF)
    tri[0] = jnp.zeros((SPN, QB), jnp.float32)
    tri[1] = jnp.where(key_at <= row_at, 0.0, LOW)
    row_max[...] = jnp.full(row_max.shape, LOW, jnp.float32)

    @pl.loop(0, 4)
    def _(q):
        acc[q] = jnp.zeros((VR, QB), jnp.float32)

    own_queries.wait()
    turn_queries(0)
    arrived_sibling(0)
    prepare(0)

    limit = limit_ref[0] * 8

    def masks(slot, q):
        chip, side = source(slot)
        row_block = jnp.where(q < 2, x, 3 - x) * 4 + core * 2 + lax.rem(q, 2)
        found = []
        for c in range(2):
            for page in range(PRE // BLK):
                number = ((chip * 2 + c) * 2 + side) * (PRE // BLK) + page
                found.append((c * PRE + page * BLK, BLK, slot_ref[number] < limit, None))
        for c in range(2):
            key_block = (chip * 2 + c) * 2 + side
            diagonal = jnp.where(key_block == row_block, 1, 0)
            found.append((2 * PRE + c * SPN, SPN, key_block <= row_block, diagonal))
        return found

    def score(slot, q, buffer):
        value = jnp.dot(k_two[slot], q_t[:, aligned(q * QB, QB)], preferred_element_type=jnp.float32)
        largest = jnp.full((1, QB), LOW, jnp.float32)
        for start, rows, visible, diagonal in masks(slot, q):
            block = value[start : start + rows]
            if diagonal is not None:
                block = block + tri[diagonal]
            scores[buffer, start : start + rows] = block
            largest = jnp.maximum(largest, jnp.where(visible, jnp.max(block, axis=0, keepdims=True), LOW))
        block_max[buffer] = largest

    def process(slot, q, buffer):
        before = row_max[q]
        now = jnp.maximum(before, block_max[buffer])
        row_max[q] = now
        weights = jnp.concatenate(
            [
                jnp.exp2(scores[buffer, start : start + rows] - jnp.where(visible, now, -LOW)).astype(jnp.bfloat16)
                for start, rows, visible, _ in masks(slot, q)
            ],
            axis=0,
        )
        added = jnp.dot(v_t[slot], weights, preferred_element_type=jnp.float32)
        acc[q] = acc[q] * jnp.exp2(before - now) + added

    def place(chip, turn, half, c):
        return heads.at[jnp.where(turn == 0, chip, 3 - chip), chip // 2, half, c]

    def moved(kind, turn, half):
        if kind < 2:
            to = device(kind + 1)
            src, dst = place(x, turn, half, core), place(chips[kind + 1], turn, half, core)
        elif kind < 4:
            to = device(kind - 1)
            rows = pl.ds((kind - 2) * (HALF // 2), HALF // 2)
            src, dst = (place(chip, turn, half, core).at[rows] for chip in (chips[4 - kind], chips[3]))
        else:
            to = sibling
            src, dst = (place(chips[kind - 4], turn, half, c) for c in (core, 1 - core))
        piece = turn * 2 + half
        make = functools.partial(
            pltpu.make_async_remote_copy, send_sem=g_send.at[piece, kind], recv_sem=g_recv.at[piece, kind],
            device_id=to, device_id_type=MESH,
        )
        return make(src_ref=src, dst_ref=src), make(src_ref=dst, dst_ref=dst)

    def send(kind, turn, half):
        moved(kind, turn, half)[0].start()

    def arrived(kind, turn, half):
        moved(kind, turn, half)[1].wait_recv()

    def finish(turn, half):
        q = turn * 2 + half
        share = 1.0 / acc[q, HD : HD + 1]
        mine = place(x, turn, half, core)
        for pair in range(8):
            at = slice(pair * HD, (pair + 1) * HD)
            block = (acc[q, :HD, at] * share[:, at]).T.astype(jnp.bfloat16)
            for one in range(2):
                mine[:, pl.ds((2 * pair + one) * HD, HD)] = block[one * HALF : (one + 1) * HALF]
        for kind in (0, 1, 4):
            send(kind, turn, half)

    def pass_on(turn, half):
        arrived(1, turn, half)
        send(2, turn, half)
        send(6, turn, half)
        arrived(0, turn, half)
        send(3, turn, half)
        send(5, turn, half)

    def pass_far(turn, half):
        arrived(2, turn, half)
        arrived(3, turn, half)
        send(7, turn, half)

    def first_part(kind):
        chip = chips[kind]
        for half in range(2):
            arrived(kind + 4, 0, half)
        depth = aligned((chip // 2) * 2048, 2048)

        @pl.loop(0, 4)
        def _(number):
            cols = aligned(number * 256, 256)
            total[chip, :, cols] = jnp.dot(
                heads[chip, chip // 2].reshape(256, 2048), weight[depth, cols], preferred_element_type=jnp.float32
            )

    def hand_on(rows, half):
        return pltpu.make_async_remote_copy(
            src_ref=part.at[rows, half], dst_ref=got.at[tp, lax.rem(rows, 2), half], send_sem=h_send.at[rows, half],
            recv_sem=h_recv.at[tp, lax.rem(rows, 2), half], device_id=(twin_section, ctx, rows // 2),
            device_id_type=MESH,
        )

    def second_part(kind, half):
        chip = chips[kind]
        rows = 3 - chip
        arrived(kind + 4, 1, half)
        depth = aligned((chip // 2) * 2048, 2048)

        @pl.loop(0, 4)
        def _(number):
            cols = aligned(number * 256, 256)
            value = jnp.dot(
                heads[rows, chip // 2, half].reshape(BLK, 2048), weight[depth, cols],
                preferred_element_type=jnp.float32,
            )
            extra = jnp.concatenate(
                [
                    rest[aligned(lax.rem(rows, 2) * 256 + c * BLK + half * HALF, HALF), cols].astype(jnp.float32)
                    for c in range(2)
                ],
                axis=0,
            )
            value = value + total[rows, pl.ds(half * BLK, BLK), cols] + jnp.where(rows // 2 == tp, extra, 0.0)
            part[rows, half, :, cols] = value.astype(jnp.bfloat16)

        hand_on(rows, half).start()

    def climb(which, half):
        return pltpu.make_async_remote_copy(
            src_ref=summed.at[which, half], dst_ref=final.at[which, half], send_sem=z_send.at[which, half],
            recv_sem=z_recv.at[which, half], device_id=(above, ctx, tp), device_id_type=MESH,
        )

    def collect(which, half):
        for side in range(2):
            ref = got.at[side, which, half]
            pltpu.make_async_remote_copy(
                src_ref=ref, dst_ref=ref, send_sem=h_send.at[which, half], recv_sem=h_recv.at[side, which, half],
                device_id=sibling, device_id_type=MESH,
            ).wait_recv()
        both = got[0, which, half].astype(jnp.float32) + got[1, which, half].astype(jnp.float32)
        summed[which, half] = both.astype(jnp.bfloat16)

        @pl.when(odd == 0)
        def _():
            climb(which, half).start()

    def step_at(number):
        slot = jnp.where(number < 16, number // 2, lax.rem(number, 8))
        return slot, jnp.where(number < 16, lax.rem(number, 2), number // 8)

    score(0, 0, 0)

    @pl.loop(0, 8)
    def _(slot):
        for at, slots in ((0, (1,)), (1, (3, 2)), (3, (5, 4)), (5, (6,)), (6, (7,))):

            @pl.when(slot == at)
            def _():
                for which in slots:
                    forward(which)
                if at == 1:
                    relay(3, 6).start()
                    row_send(5).start()
                    row_send(4).start()
                    swap.start()
                if at == 3:
                    relay(5, 7).start()

        @pl.when(slot < 7)
        def _():
            arrived_sibling(slot + 1)

        prepare(jnp.minimum(slot + 1, 7))
        score(slot, 1, 1)
        process(slot, 0, 0)

        @pl.when(slot == 7)
        def _():
            swap.wait_recv()
            turn_queries(1)

        score(*step_at(2 * slot + 2), 0)
        process(slot, 1, 1)

    for half in range(2):
        finish(0, half)

    @pl.loop(8, 16)
    def _(turn):
        @pl.when(turn == 11)
        def _():
            pass_on(0, 0)

        @pl.when(turn == 13)
        def _():
            pass_on(0, 1)

        @pl.when(turn == 14)
        def _():
            first_part(2)
            second_part(0, 0)

        score(*step_at(2 * turn + 1), 1)
        process(*step_at(2 * turn), 0)
        score(*step_at(jnp.minimum(2 * turn + 2, 31)), 0)
        process(*step_at(2 * turn + 1), 1)

        @pl.when(turn == 11)
        def _():
            finish(1, 0)

        @pl.when(turn == 10)
        def _():
            load_weight.wait()
            load_rest.wait()

    finish(1, 1)
    for half in range(2):
        pass_far(0, half)
    first_part(0)
    pass_on(1, 0)
    second_part(0, 1)
    second_part(2, 0)
    first_part(3)
    second_part(1, 0)
    first_part(1)
    pass_on(1, 1)
    pass_far(1, 0)
    second_part(3, 0)
    second_part(2, 1)
    second_part(1, 1)
    early = jnp.where(tp == (3 - x) // 2, lax.rem(3 - x, 2), lax.rem(x, 2))
    collect(early, 0)
    pass_far(1, 1)
    second_part(3, 1)
    collect(1 - early, 0)
    collect(early, 1)
    collect(1 - early, 1)

    def write(ref, which, half):
        for c in range(2):
            out_ref[aligned(which * 256 + c * BLK + half * HALF, HALF)] = ref[which, half, pl.ds(c * HALF, HALF)]

    @pl.loop(0, 4)
    def _(number):
        which, half = number // 2, lax.rem(number, 2)

        @pl.when(odd == 0)
        def _():
            climb(which, half).wait_recv()
            write(final, which, half)

        @pl.when(odd == 1)
        def _():
            write(summed, which, half)

    for slot in range(1, 6):
        row_send(slot).wait_send()
    relay(3, 6).wait_send()
    relay(5, 7).wait_send()
    swap.wait_send()

    @pl.loop(0, 8)
    def _(slot):
        to_sibling(slot).wait_send()

    @pl.loop(0, 4)
    def _(piece):
        for kind in range(8):
            moved(kind, piece // 2, lax.rem(piece, 2))[0].wait_send()

        for half in range(2):
            hand_on(piece, half).wait_send()

        @pl.when(odd == 0)
        def _():
            climb(piece // 2, lax.rem(piece, 2)).wait_send()


def layer(
    queries, span_keys, span_values, prefix_keys, prefix_values, out_weight, residual, block_slot, span_index
):
    any_spec = pl.BlockSpec(memory_space=pl.ANY)
    smem = pl.BlockSpec(memory_space=pltpu.SMEM)
    vmem = pl.BlockSpec(memory_space=pltpu.VMEM)
    dma = pltpu.SemaphoreType.DMA
    bf16, f32 = jnp.bfloat16, jnp.float32
    return pl.pallas_call(
        layer_kernel,
        out_shape=jax.ShapeDtypeStruct((512, 1024), bf16),
        in_specs=[any_spec] * 7 + [smem, smem],
        out_specs=vmem,
        scratch_shapes=[
            pltpu.VMEM((4, 2, 2, 2, HALF, 2048), bf16),
            pltpu.VMEM((4096, 1024), bf16),
            pltpu.VMEM((512, 1024), bf16),
            pltpu.VMEM((4, 256, 1024), f32),
            pltpu.VMEM((4, 2, BLK, 1024), bf16),
            pltpu.VMEM((2, 2, 2, BLK, 1024), bf16),
            pltpu.VMEM((2, 2, BLK, 1024), bf16),
            pltpu.VMEM((2, 2, BLK, 1024), bf16),
            pltpu.VMEM((3, 2, ROWS, HD), bf16),
            pltpu.VMEM((8, 2, 2, ROWS, HD), bf16),
            pltpu.VMEM((2, BLK, 2048), bf16),
            pltpu.VMEM((2 * HD, 4 * QB), bf16),
            pltpu.VMEM((8, SLOT, 2 * HD), bf16),
            pltpu.VMEM((8, VR, SLOT), bf16),
            pltpu.VMEM((2, SLOT, QB), f32),
            pltpu.VMEM((2, SPN, QB), f32),
            pltpu.VMEM((2, 1, QB), f32),
            pltpu.VMEM((4, 1, QB), f32),
            pltpu.VMEM((4, VR, QB), f32),
            dma((4,)), dma((3,)), dma((6,)), dma((8,)), dma((8,)), dma((8,)), dma((2,)), dma(()), dma(()),
            dma((4, 8)), dma((4, 8)), dma((4, 2)), dma((2, 2, 2)), dma((2, 2)), dma((2, 2)),
        ],
        compiler_params=pltpu.CompilerParams(
            collective_id=0, has_side_effects=True, vmem_limit_bytes=60 << 20
        ),
        name="layer",
    )(
        queries, span_keys, span_values, prefix_keys, prefix_values, out_weight, residual, block_slot, span_index
    )


def per_device(
    queries, span_keys, span_values, prefix_keys, prefix_values, out_weight, residual, block_slot, span_index
):
    return layer(
        queries[0], span_keys[0], span_values[0], prefix_keys[0], prefix_values[0], out_weight[0], residual[0],
        block_slot, span_index,
    )[None]


def solution(mesh):
    in_specs = (
        P("section", "ctx", "tp"),
        P("section", ("ctx", "tp"), None),
        P("section", ("ctx", "tp"), None),
        P("section", ("ctx", "tp"), None),
        P("section", ("ctx", "tp"), None),
        P("section", "tp", "ctx"),
        P("section", "tp", "ctx"),
        P(),
        P("section"),
    )
    return jax.shard_map(
        per_device, mesh=mesh, in_specs=in_specs, out_specs=P("section", "tp", "ctx"), check_vma=False
    )
```

time: 225 us -> 121 us (0.54)
  waiting for transfers between devices: 113 us -> 0 us
  Pallas kernels: 77.6 us -> 118 us
  between operations: 14.2 us -> 0.66 us
  matrix products: 10.1 us -> 0 us
  local copies, waits for them, and re-layouts: 7.55 us -> 2.26 us
  other arithmetic: 2.34 us -> 0 us
    all_gather x1 -> x0, waiting for transfers between devices: 51 us -> none  [per_device(): every = lax.all_gather(heads, 'ctx', axis=0)]
    pallas_call x1, Pallas kernels: 77.6 us -> 118 us  [layer(): pl.pallas_call(layer_kernel, out_shape=jax.ShapeDtypeStruct((512, 1024),...]
    reduce_scatter x1 -> x0, waiting for transfers between devices: 35.8 us -> none  [per_device(): lax.psum_scatter(partial.astype(jnp.bfloat16), 'tp', scatter_dimension=0,...]
    ppermute x1 -> x0, waiting for transfers between devices: 25.8 us -> none  [per_device(): lax.ppermute(layer, 'section', [(i, (i + 1) % sections) for i in range(se...]
    dot_general x1 -> x0, matrix products: 10.1 us -> none  [per_device(): jnp.dot(jnp.concatenate(rows, axis=0), out_weight[0], preferred_element_t...]
    squeeze x1 -> x0, local copies, waits for them, and re-layouts: 3.8 us -> none  [per_device(): pair = (every[ctx, 0], every[other, 1])]
  transfers between devices with their start and end apart: 3 -> 0, of which waited for: 3 -> 0; matrix products, arithmetic and copies ran while one was open for 0% -> 0% of each run, Pallas kernels for 0% -> 0%
where the time goes in v3:
time: 121 us
  Pallas kernels  118 us (98%)
  local copies, waits for them, and re-layouts  2.26 us (2%)
    pallas_call x1, Pallas kernels, layer(): pl.pallas_call(layer_kernel, out_shape=jax.ShapeDtypeStruct((512, 1024),...  118 us

profile of v3, /device:TPU:1, one launch (start us, length us, event | category | flops | bytes accessed | tf_op | source)
XLA Modules:
  0.0 121.1 jit_solution(17674177021285377563)
XLA Ops:
  0.7 118.2 %layer.1 = bf16[512,1024]{1,0:T(8,128)(2,1)} custom-call(bf16[128,4096]{1,0:T(8,128)(2,1)} %bitcast.10, bf16[64,512]{1,0:T(8,128)(2,1)} %bitcast.14, bf16[64,512]{1,0:T(8,128)(2,1)} %bitcast.15, bf16[384,512]{1,0:T(8,128)(2,1)} %bitcast.12, bf16[384,512]{1,0:T(8,128)(2,1)} %bitcast.13, bf16[4096,1024]{1,0:T(8,128)(2,1)} %bitcast.8, ...), custom_call_target="tpu_custom_call" | custom-call | tf_op jit(solution)/shard_map/layer/pallas_call | solution.py:476
  118.9 2.3 %copy.12 = bf16[1,512,1024]{2,1,0:T(8,128)(2,1)} copy(bf16[1,512,1024]{2,1,0:T(8,128)(2,1)} %bitcast.9) | data formatting | bytes 2097152

commit v4 on v3

--- a/solution.py
+++ b/solution.py
@@ -19,7 +19,8 @@
 SLOT = 2 * ROWS
 VR = 144
 LOW = -1e30
-SLOTS = ((0, 0), (0, 1), (1, 0), (2, 0), (1, 1), (2, 1), (3, 0), (3, 1))
+SLOTS = ((0, 0), (1, 0), (2, 0), (0, 1), (1, 1), (3, 0), (2, 1), (3, 1))
+SENT = (1, 2, 3, 4, 6)
 
 
 def pick(index, table):
@@ -55,7 +56,7 @@
     above, below = lax.rem(section + 2, 8), lax.rem(section + 6, 8)
 
     barrier = pltpu.get_barrier_semaphore()
-    greeted = [device(kind, dt) for kind, dt in SLOTS[1:6]] + [sibling]
+    greeted = [device(*SLOTS[slot]) for slot in SENT] + [sibling]
     greeted += [(twin_section, ctx, half) for half in range(2)] + [(below, ctx, tp)]
     for other in greeted:
         pl.semaphore_signal(barrier, inc=1, device_id=other, device_id_type=MESH)
@@ -91,7 +92,7 @@
 
     def relay(slot, to):
         return pltpu.make_async_remote_copy(
-            src_ref=kv.at[slot, core], dst_ref=kv.at[to, core], send_sem=relay_send.at[to - 6],
+            src_ref=kv.at[slot, core], dst_ref=kv.at[to, core], send_sem=relay_send.at[to // 7],
             recv_sem=recv_sem.at[to], device_id=device(1), device_id_type=MESH,
         )
 
@@ -115,7 +116,7 @@
     for number in range(4):
         wait_block(number)
     pl.semaphore_wait(barrier, len(greeted))
-    for slot in (3, 2, 1):
+    for slot in (2, 1, 3):
         row_send(slot).start()
     to_sibling(0).start()
     load_weight = pltpu.make_async_copy(w_hbm, weight, local_sem.at[1])
@@ -251,6 +252,8 @@
             block = (acc[q, :HD, at] * share[:, at]).T.astype(jnp.bfloat16)
             for one in range(2):
                 mine[:, pl.ds((2 * pair + one) * HD, HD)] = block[one * HALF : (one + 1) * HALF]
+
+    def publish(turn, half):
         for kind in (0, 1, 4):
             send(kind, turn, half)
 
@@ -273,18 +276,18 @@
             arrived(kind + 4, 0, half)
         depth = aligned((chip // 2) * 2048, 2048)
 
-        @pl.loop(0, 4)
+        @pl.loop(0, 2)
         def _(number):
-            cols = aligned(number * 256, 256)
+            cols = aligned(number * 512, 512)
             total[chip, :, cols] = jnp.dot(
                 heads[chip, chip // 2].reshape(256, 2048), weight[depth, cols], preferred_element_type=jnp.float32
             )
 
-    def hand_on(rows, half):
+    def hand_on(rows, half, side):
+        here = (tp, lax.rem(rows, 2), half, side)
         return pltpu.make_async_remote_copy(
-            src_ref=part.at[rows, half], dst_ref=got.at[tp, lax.rem(rows, 2), half], send_sem=h_send.at[rows, half],
-            recv_sem=h_recv.at[tp, lax.rem(rows, 2), half], device_id=(twin_section, ctx, rows // 2),
-            device_id_type=MESH,
+            src_ref=part.at[rows, half, side], dst_ref=got.at[here], send_sem=h_send.at[rows, half, side],
+            recv_sem=h_recv.at[here], device_id=(twin_section, ctx, rows // 2), device_id_type=MESH,
         )
 
     def second_part(kind, half):
@@ -293,9 +296,9 @@
         arrived(kind + 4, 1, half)
         depth = aligned((chip // 2) * 2048, 2048)
 
-        @pl.loop(0, 4)
+        @pl.loop(0, 2)
         def _(number):
-            cols = aligned(number * 256, 256)
+            cols = aligned(number * 512, 512)
             value = jnp.dot(
                 heads[rows, chip // 2, half].reshape(BLK, 2048), weight[depth, cols],
                 preferred_element_type=jnp.float32,
@@ -308,29 +311,32 @@
                 axis=0,
             )
             value = value + total[rows, pl.ds(half * BLK, BLK), cols] + jnp.where(rows // 2 == tp, extra, 0.0)
-            part[rows, half, :, cols] = value.astype(jnp.bfloat16)
-
-        hand_on(rows, half).start()
-
-    def climb(which, half):
+            part[rows, half, number] = value.astype(jnp.bfloat16)
+            hand_on(rows, half, number).start()
+
+    def climb(unit):
         return pltpu.make_async_remote_copy(
-            src_ref=summed.at[which, half], dst_ref=final.at[which, half], send_sem=z_send.at[which, half],
-            recv_sem=z_recv.at[which, half], device_id=(above, ctx, tp), device_id_type=MESH,
+            src_ref=summed.at[unit], dst_ref=final.at[unit], send_sem=z_send.at[unit], recv_sem=z_recv.at[unit],
+            device_id=(above, ctx, tp), device_id_type=MESH,
         )
 
     def collect(which, half):
-        for side in range(2):
-            ref = got.at[side, which, half]
-            pltpu.make_async_remote_copy(
-                src_ref=ref, dst_ref=ref, send_sem=h_send.at[which, half], recv_sem=h_recv.at[side, which, half],
-                device_id=sibling, device_id_type=MESH,
-            ).wait_recv()
-        both = got[0, which, half].astype(jnp.float32) + got[1, which, half].astype(jnp.float32)
-        summed[which, half] = both.astype(jnp.bfloat16)
-
-        @pl.when(odd == 0)
-        def _():
-            climb(which, half).start()
+        @pl.loop(0, 2)
+        def _(side):
+            unit = (which, half, side)
+            for origin in range(2):
+                place_of = (origin, *unit)
+                ref = got.at[place_of]
+                pltpu.make_async_remote_copy(
+                    src_ref=ref, dst_ref=ref, send_sem=h_send.at[unit], recv_sem=h_recv.at[place_of],
+                    device_id=sibling, device_id_type=MESH,
+                ).wait_recv()
+            both = got[(0, *unit)].astype(jnp.float32) + got[(1, *unit)].astype(jnp.float32)
+            summed[unit] = both.astype(jnp.bfloat16)
+
+            @pl.when(odd == 0)
+            def _():
+                climb(unit).start()
 
     def step_at(number):
         slot = jnp.where(number < 16, number // 2, lax.rem(number, 8))
@@ -340,42 +346,47 @@
 
     @pl.loop(0, 8)
     def _(slot):
-        for at, slots in ((0, (1,)), (1, (3, 2)), (3, (5, 4)), (5, (6,)), (6, (7,))):
+        for at, slots in ((2, (3,)), (3, (6, 4)), (4, (5,)), (6, (7,))):
 
             @pl.when(slot == at)
             def _():
                 for which in slots:
                     forward(which)
-                if at == 1:
-                    relay(3, 6).start()
-                    row_send(5).start()
-                    row_send(4).start()
-                    swap.start()
-                if at == 3:
-                    relay(5, 7).start()
-
-        @pl.when(slot < 7)
-        def _():
-            arrived_sibling(slot + 1)
-
-        prepare(jnp.minimum(slot + 1, 7))
+                    if which == 6:
+                        relay(6, 7).start()
+
         score(slot, 1, 1)
         process(slot, 0, 0)
 
+        @pl.when(slot == 0)
+        def _():
+            forward(1)
+            forward(2)
+            relay(2, 5).start()
+            row_send(6).start()
+            row_send(4).start()
+            swap.start()
+
+        @pl.when(slot < 7)
+        def _():
+            arrived_sibling(slot + 1)
+
         @pl.when(slot == 7)
         def _():
             swap.wait_recv()
             turn_queries(1)
 
+        prepare(jnp.minimum(slot + 1, 7))
         score(*step_at(2 * slot + 2), 0)
         process(slot, 1, 1)
 
     for half in range(2):
         finish(0, half)
+        publish(0, half)
 
     @pl.loop(8, 16)
     def _(turn):
-        @pl.when(turn == 11)
+        @pl.when(turn == 12)
         def _():
             pass_on(0, 0)
 
@@ -396,6 +407,7 @@
         @pl.when(turn == 11)
         def _():
             finish(1, 0)
+            publish(1, 0)
 
         @pl.when(turn == 10)
         def _():
@@ -407,45 +419,49 @@
         pass_far(0, half)
     first_part(0)
     pass_on(1, 0)
-    second_part(0, 1)
+    publish(1, 1)
     second_part(2, 0)
     first_part(3)
     second_part(1, 0)
     first_part(1)
-    pass_on(1, 1)
     pass_far(1, 0)
     second_part(3, 0)
+    second_part(0, 1)
+    early = jnp.where(tp == (3 - x) // 2, lax.rem(3 - x, 2), lax.rem(x, 2))
+    collect(early, 0)
+    pass_on(1, 1)
     second_part(2, 1)
     second_part(1, 1)
-    early = jnp.where(tp == (3 - x) // 2, lax.rem(3 - x, 2), lax.rem(x, 2))
-    collect(early, 0)
+    collect(1 - early, 0)
     pass_far(1, 1)
     second_part(3, 1)
-    collect(1 - early, 0)
     collect(early, 1)
     collect(1 - early, 1)
 
-    def write(ref, which, half):
+    def write(ref, unit):
+        which, half, side = unit
         for c in range(2):
-            out_ref[aligned(which * 256 + c * BLK + half * HALF, HALF)] = ref[which, half, pl.ds(c * HALF, HALF)]
-
-    @pl.loop(0, 4)
+            rows = aligned(which * 256 + c * BLK + half * HALF, HALF)
+            out_ref[rows, aligned(side * 512, 512)] = ref[(*unit, pl.ds(c * HALF, HALF))]
+
+    @pl.loop(0, 8)
     def _(number):
-        which, half = number // 2, lax.rem(number, 2)
+        half, which, side = number // 4, lax.rem(number // 2, 2), lax.rem(number, 2)
+        unit = (which, half, side)
 
         @pl.when(odd == 0)
         def _():
-            climb(which, half).wait_recv()
-            write(final, which, half)
+            climb(unit).wait_recv()
+            write(final, unit)
 
         @pl.when(odd == 1)
         def _():
-            write(summed, which, half)
-
-    for slot in range(1, 6):
+            write(summed, unit)
+
+    for slot in SENT:
         row_send(slot).wait_send()
-    relay(3, 6).wait_send()
-    relay(5, 7).wait_send()
+    relay(2, 5).wait_send()
+    relay(6, 7).wait_send()
     swap.wait_send()
 
     @pl.loop(0, 8)
@@ -458,11 +474,13 @@
             moved(kind, piece // 2, lax.rem(piece, 2))[0].wait_send()
 
         for half in range(2):
-            hand_on(piece, half).wait_send()
+            for side in range(2):
+                hand_on(piece, half, side).wait_send()
 
         @pl.when(odd == 0)
         def _():
-            climb(piece // 2, lax.rem(piece, 2)).wait_send()
+            for side in range(2):
+                climb((piece // 2, lax.rem(piece, 2), side)).wait_send()
 
 
 def layer(
@@ -483,10 +501,10 @@
             pltpu.VMEM((4096, 1024), bf16),
             pltpu.VMEM((512, 1024), bf16),
             pltpu.VMEM((4, 256, 1024), f32),
-            pltpu.VMEM((4, 2, BLK, 1024), bf16),
-            pltpu.VMEM((2, 2, 2, BLK, 1024), bf16),
-            pltpu.VMEM((2, 2, BLK, 1024), bf16),
-            pltpu.VMEM((2, 2, BLK, 1024), bf16),
+            pltpu.VMEM((4, 2, 2, BLK, 512), bf16),
+            pltpu.VMEM((2, 2, 2, 2, BLK, 512), bf16),
+            pltpu.VMEM((2, 2, 2, BLK, 512), bf16),
+            pltpu.VMEM((2, 2, 2, BLK, 512), bf16),
             pltpu.VMEM((3, 2, ROWS, HD), bf16),
             pltpu.VMEM((8, 2, 2, ROWS, HD), bf16),
             pltpu.VMEM((2, BLK, 2048), bf16),
@@ -498,8 +516,8 @@
             pltpu.VMEM((2, 1, QB), f32),
             pltpu.VMEM((4, 1, QB), f32),
             pltpu.VMEM((4, VR, QB), f32),
-            dma((4,)), dma((3,)), dma((6,)), dma((8,)), dma((8,)), dma((8,)), dma((2,)), dma(()), dma(()),
-            dma((4, 8)), dma((4, 8)), dma((4, 2)), dma((2, 2, 2)), dma((2, 2)), dma((2, 2)),
+            dma((4,)), dma((3,)), dma((8,)), dma((8,)), dma((8,)), dma((8,)), dma((2,)), dma(()), dma(()),
+            dma((4, 8)), dma((4, 8)), dma((4, 2, 2)), dma((2, 2, 2, 2)), dma((2, 2, 2)), dma((2, 2, 2)),
         ],
         compiler_params=pltpu.CompilerParams(
             collective_id=0, has_side_effects=True, vmem_limit_bytes=60 << 20

time: 121 us -> 109 us (0.901)
  Pallas kernels: 118 us -> 106 us
    pallas_call x1, Pallas kernels: 118 us -> 106 us  [layer(): pl.pallas_call(layer_kernel, out_shape=jax.ShapeDtypeStruct((512, 1024),...]
where the time goes in v4:
time: 109 us
  Pallas kernels  106 us (97%)
  local copies, waits for them, and re-layouts  2.26 us (2%)
    pallas_call x1, Pallas kernels, layer(): pl.pallas_call(layer_kernel, out_shape=jax.ShapeDtypeStruct((512, 1024),...  106 us
    unnamed x1, local copies, waits for them, and re-layouts  2.26 us

profile of v4, /device:TPU:1, one launch (start us, length us, event | category | flops | bytes accessed | tf_op | source)
XLA Modules:
  0.0 108.9 jit_solution(16344671588053658320)
XLA Ops:
  0.7 106.0 %layer.1 = bf16[512,1024]{1,0:T(8,128)(2,1)} custom-call(bf16[128,4096]{1,0:T(8,128)(2,1)} %bitcast.10, bf16[64,512]{1,0:T(8,128)(2,1)} %bitcast.14, bf16[64,512]{1,0:T(8,128)(2,1)} %bitcast.15, bf16[384,512]{1,0:T(8,128)(2,1)} %bitcast.12, bf16[384,512]{1,0:T(8,128)(2,1)} %bitcast.13, bf16[4096,1024]{1,0:T(8,128)(2,1)} %bitcast.8, ...), custom_call_target="tpu_custom_call" | custom-call | tf_op jit(solution)/shard_map/layer/pallas_call | solution.py:494
  106.7 2.3 %copy.12 = bf16[1,512,1024]{2,1,0:T(8,128)(2,1)} copy(bf16[1,512,1024]{2,1,0:T(8,128)(2,1)} %bitcast.9) | data formatting | bytes 2097152

commit v5 on v4

--- a/solution.py
+++ b/solution.py
@@ -39,7 +39,7 @@
     heads, weight, rest, total, part, got, summed, final, stage, kv, q_raw, q_t, k_two, v_t, scores, tri,
     block_max, row_max, acc,
     stage_sem, local_sem, send_sem, recv_sem, fwd_send, fwd_recv, relay_send, q_send, q_recv,
-    g_send, g_recv, h_send, h_recv, z_send, z_recv,
+    g_send, g_recv, h_send, h_recv, z_send, z_recv, out_sem,
 ):
     section, ctx, tp = lax.axis_index("section"), lax.axis_index("ctx"), lax.axis_index("tp")
     x, core = ctx // 2, lax.rem(ctx, 2)
@@ -116,7 +116,7 @@
     for number in range(4):
         wait_block(number)
     pl.semaphore_wait(barrier, len(greeted))
-    for slot in (2, 1, 3):
+    for slot in (2, 1, 6, 3):
         row_send(slot).start()
     to_sibling(0).start()
     load_weight = pltpu.make_async_copy(w_hbm, weight, local_sem.at[1])
@@ -363,26 +363,27 @@
             forward(1)
             forward(2)
             relay(2, 5).start()
-            row_send(6).start()
             row_send(4).start()
             swap.start()
 
         @pl.when(slot < 7)
         def _():
             arrived_sibling(slot + 1)
+            prepare(slot + 1)
+            score(slot + 1, 0, 0)
+            process(slot, 1, 1)
 
         @pl.when(slot == 7)
         def _():
-            swap.wait_recv()
-            turn_queries(1)
-
-        prepare(jnp.minimum(slot + 1, 7))
-        score(*step_at(2 * slot + 2), 0)
-        process(slot, 1, 1)
-
-    for half in range(2):
-        finish(0, half)
-        publish(0, half)
+            finish(0, 0)
+            publish(0, 0)
+            process(slot, 1, 1)
+
+    finish(0, 1)
+    publish(0, 1)
+    swap.wait_recv()
+    turn_queries(1)
+    score(0, 2, 0)
 
     @pl.loop(8, 16)
     def _(turn):
@@ -440,23 +441,39 @@
 
     def write(ref, unit):
         which, half, side = unit
+        copies = []
         for c in range(2):
             rows = aligned(which * 256 + c * BLK + half * HALF, HALF)
-            out_ref[rows, aligned(side * 512, 512)] = ref[(*unit, pl.ds(c * HALF, HALF))]
+            copies.append(
+                pltpu.make_async_copy(
+                    ref.at[(*unit, pl.ds(c * HALF, HALF))], out_ref.at[rows, aligned(side * 512, 512)],
+                    out_sem.at[(*unit, c)],
+                )
+            )
+        return copies
+
+    def unit_of(number):
+        return (lax.rem(number // 2, 2), number // 4, lax.rem(number, 2))
 
     @pl.loop(0, 8)
     def _(number):
-        half, which, side = number // 4, lax.rem(number // 2, 2), lax.rem(number, 2)
-        unit = (which, half, side)
+        unit = unit_of(number)
 
         @pl.when(odd == 0)
         def _():
             climb(unit).wait_recv()
-            write(final, unit)
+            for copy in write(final, unit):
+                copy.start()
 
         @pl.when(odd == 1)
         def _():
-            write(summed, unit)
+            for copy in write(summed, unit):
+                copy.start()
+
+    @pl.loop(0, 8)
+    def _(number):
+        for copy in write(final, unit_of(number)):
+            copy.wait()
 
     for slot in SENT:
         row_send(slot).wait_send()
@@ -488,14 +505,13 @@
 ):
     any_spec = pl.BlockSpec(memory_space=pl.ANY)
     smem = pl.BlockSpec(memory_space=pltpu.SMEM)
-    vmem = pl.BlockSpec(memory_space=pltpu.VMEM)
     dma = pltpu.SemaphoreType.DMA
     bf16, f32 = jnp.bfloat16, jnp.float32
     return pl.pallas_call(
         layer_kernel,
         out_shape=jax.ShapeDtypeStruct((512, 1024), bf16),
         in_specs=[any_spec] * 7 + [smem, smem],
-        out_specs=vmem,
+        out_specs=any_spec,
         scratch_shapes=[
             pltpu.VMEM((4, 2, 2, 2, HALF, 2048), bf16),
             pltpu.VMEM((4096, 1024), bf16),
@@ -518,6 +534,7 @@
             pltpu.VMEM((4, VR, QB), f32),
             dma((4,)), dma((3,)), dma((8,)), dma((8,)), dma((8,)), dma((8,)), dma((2,)), dma(()), dma(()),
             dma((4, 8)), dma((4, 8)), dma((4, 2, 2)), dma((2, 2, 2, 2)), dma((2, 2, 2)), dma((2, 2, 2)),
+            dma((2, 2, 2, 2)),
         ],
         compiler_params=pltpu.CompilerParams(
             collective_id=0, has_side_effects=True, vmem_limit_bytes=60 << 20

time: 109 us -> 106 us (0.972)
  Pallas kernels: 106 us -> 103 us
    pallas_call x1, Pallas kernels: 106 us -> 103 us  [layer(): pl.pallas_call(layer_kernel, out_shape=jax.ShapeDtypeStruct((512, 1024),...]
where the time goes in v5:
time: 106 us
  Pallas kernels  103 us (97%)
  local copies, waits for them, and re-layouts  2.26 us (2%)
    pallas_call x1, Pallas kernels, layer(): pl.pallas_call(layer_kernel, out_shape=jax.ShapeDtypeStruct((512, 1024),...  103 us
    unnamed x1, local copies, waits for them, and re-layouts  2.26 us

profile of v5, /device:TPU:1, one launch (start us, length us, event | category | flops | bytes accessed | tf_op | source)
XLA Modules:
  0.0 105.6 jit_solution(12002299365380421662)
XLA Ops:
  0.7 102.7 %layer.1 = bf16[512,1024]{1,0:T(8,128)(2,1)} custom-call(bf16[128,4096]{1,0:T(8,128)(2,1)} %bitcast.10, bf16[64,512]{1,0:T(8,128)(2,1)} %bitcast.14, bf16[64,512]{1,0:T(8,128)(2,1)} %bitcast.15, bf16[384,512]{1,0:T(8,128)(2,1)} %bitcast.12, bf16[384,512]{1,0:T(8,128)(2,1)} %bitcast.13, bf16[4096,1024]{1,0:T(8,128)(2,1)} %bitcast.8, ...), custom_call_target="tpu_custom_call" | custom-call | tf_op jit(solution)/shard_map/layer/pallas_call | solution.py:510
  103.4 2.3 %copy.12 = bf16[1,512,1024]{2,1,0:T(8,128)(2,1)} copy(bf16[1,512,1024]{2,1,0:T(8,128)(2,1)} %bitcast.9) | data formatting | bytes 2097152
